TPU v7x, 32 devices: a whole 2x2x4 slice. The times are simulated.
32 devices in a mesh: dp: 16 (over z, y, x), expert: 2 (over core).
Axes of the slice: x: 2, y: 2, z: 4, core: 2. Of those that a mesh axis runs over, the one named last changes fastest.
Arguments:
- inputs: bfloat16 [32768, 512], P(('dp', 'expert')), may hold values from -6 to 6
- cotangent: bfloat16 [32768, 512], P(('dp', 'expert')), may hold values from -6 to 6
- lengths: int32 [16, 2, 4], P('dp'), may hold values from 0 to 1024, as said below
- routes: int32 [16, 2, 1024, 2], P('dp'), may hold values from 0 to 7, all different within a row; in each aligned block of 1024 rows (0 to 1023, 1024 to 2047, ..., all dimensions but the last counted through in order) at most 512 rows name the same one
- first_gain: bfloat16 [512], replicated, may hold values from 0.5 to 1.5
- first_bias: bfloat16 [512], replicated, may hold values from -1.1953125 to 1.1953125
- router_weight: bfloat16 [512, 8], replicated, may hold values from -0.25 to 0.25
- key_weight: bfloat16 [512, 64], replicated, may hold values from -0.25 to 0.25
- value_weight: bfloat16 [512, 64], replicated, may hold values from -0.25 to 0.25
- query_weight: bfloat16 [8, 512, 64], P('expert'), may hold values from -0.25 to 0.25
- output_weight: bfloat16 [8, 64, 512], P('expert'), may hold values from -3 to 3
- second_gain: bfloat16 [512], replicated, may hold values from 0.5 to 1.5
- second_bias: bfloat16 [512], replicated, may hold values from -1.1953125 to 1.1953125
- hidden_weight: bfloat16 [512, 2048], replicated, may hold values from -0.25 to 0.25
- hidden_bias: bfloat16 [2048], replicated, may hold values from -1.1953125 to 1.1953125
- return_weight: bfloat16 [2048, 512], replicated, may hold values from -0.25 to 0.25
- return_bias: bfloat16 [512], replicated, may hold values from -1.1953125 to 1.1953125
Outputs:
- layer_out: float32 [32768, 512], P(('dp', 'expert'))
- input_grad: float32 [32768, 512], P(('dp', 'expert'))
- first_gain_grad: float32 [512], replicated
- first_bias_grad: float32 [512], replicated
- router_grad: float32 [512, 8], replicated
- key_grad: float32 [512, 64], replicated
- value_grad: float32 [512, 64], replicated
- query_grad: float32 [8, 512, 64], P('expert')
- output_grad: float32 [8, 64, 512], P('expert')
- second_gain_grad: float32 [512], replicated
- second_bias_grad: float32 [512], replicated
- hidden_grad: float32 [512, 2048], replicated
- hidden_bias_grad: float32 [2048], replicated
- return_grad: float32 [2048, 512], replicated
- return_bias_grad: float32 [512], replicated
Inputs may be any that keep to these rules, and one draw needn't show every extreme that they name: Slots with length 0 are unused; a device's lengths sum to at most 1024 and the rest of its rows are padding; devices hold different numbers of sentences; in every draw some device holds a single sentence of 1024 rows. Each token names two different experts; the rows of one device name no expert more than 512 times, and in every draw some device names some expert exactly 512 times. routes[i, j] belongs to the device at index i of dp and j of expert.
All inputs are finite; a program needn't handle non-finite values.
Results may differ from a plain program's by a relative error of at most 0.012.
Values may be sent and summed in bfloat16 or wider, within the bound.
No kernel may reach another device: no remote copies, remote signals or barrier semaphores. Data moves between devices by JAX's collectives and lax.ppermute only.
A program may use at most 192 MiB of HBM per device.

v0:
```python
import functools

import jax
import jax.numpy as jnp
from jax import lax
from jax.experimental import pallas as pl
from jax.experimental.pallas import tpu as pltpu
from jax.sharding import PartitionSpec as P

AXES = ("dp", "expert")
WIDE = jnp.float32
LOW = jnp.bfloat16
EPS = 1e-05
MASKED = -1e30
REACH = 40.0
ROWS = 256
SPAN = 512
CURVE = 0.7978845608028654
CUBIC = 0.044715
VMEM_LIMIT = 16 * 1024 * 1024


def low(values):
    return values.astype(LOW)


def wide(values):
    return values.astype(WIDE)


def dot_nn(left_op, right_op):
    return lax.dot_general(
        left_op, right_op, (((1,), (0,)), ((), ())), preferred_element_type=WIDE
    )


def dot_tn(left_op, right_op):
    return lax.dot_general(
        left_op, right_op, (((0,), (0,)), ((), ())), preferred_element_type=WIDE
    )


def dot_nt(left_op, right_op):
    return lax.dot_general(
        left_op, right_op, (((1,), (1,)), ((), ())), preferred_element_type=WIDE
    )


def norm_parts(values):
    row_mean = jnp.mean(values, axis=-1, keepdims=True)
    centred = values - row_mean
    inv_dev = lax.rsqrt(jnp.mean(centred * centred, axis=-1, keepdims=True) + EPS)
    return centred * inv_dev, inv_dev


def norm_back(d_out, unit, inv_dev, gain_vec):
    weighted = d_out * gain_vec
    mean_w = jnp.mean(weighted, axis=-1, keepdims=True)
    mean_wn = jnp.mean(weighted * unit, axis=-1, keepdims=True)
    return inv_dev * (weighted - mean_w - unit * mean_wn)


def core_here():
    return lax.axis_index("expert")


def segment_of(places, ends):
    return sum((places >= end).astype(jnp.int32) for end in ends)


def held(shape, dtype):
    return pltpu.VMEM(shape, dtype)


def there(shape, dtype):
    return jax.ShapeDtypeStruct(shape, dtype)


ANYWHERE = pl.BlockSpec(memory_space=pl.ANY)
INSIDE = pl.BlockSpec(memory_space=pltpu.VMEM)


class Program:
    def __init__(self):
        self.before = []

    def call(self, kernel, name, operands, out_shape, scratch=(), far=(), far_out=0, aliases=()):
        operands = [pltpu.with_memory_space_constraint(v, pltpu.VMEM) for v in operands]
        if not aliases:
            far = [pltpu.with_memory_space_constraint(v, pltpu.HBM) for v in far]
        count, waits = len(operands) + len(far), len(self.before)

        def run(*refs):
            kernel(*refs[:count], *refs[count + waits :])

        single = not isinstance(out_shape, (list, tuple))
        outs = [out_shape] if single else list(out_shape)
        near = len(outs) - far_out
        result = pl.pallas_call(
            run,
            in_specs=[INSIDE] * len(operands) + [ANYWHERE] * (len(far) + waits),
            out_specs=[INSIDE] * near + [ANYWHERE] * far_out,
            out_shape=outs,
            scratch_shapes=list(scratch),
            input_output_aliases={len(operands) + a: near + b for a, b in aliases},
            compiler_params=pltpu.CompilerParams(vmem_limit_bytes=VMEM_LIMIT),
            cost_estimate=pl.CostEstimate(flops=3 * 10**10 if name == "rest_add_1" else 10**10, bytes_accessed=1, transcendentals=0),
            name=name,
        )(*operands, *far, *self.before)
        self.before = [result[0]]
        return result[0] if single else result


FIRST_GAIN, FIRST_BIAS, SECOND_GAIN, SECOND_BIAS, RETURN_BIAS, HIDDEN_BIAS = range(6)
SLOTS = 4
PARTS = 8


def bias_row(vecs, unit, cols):
    row = vecs[pl.ds(HIDDEN_BIAS + unit // 2, 1), :]
    return jnp.where(unit % 2 == 0, row[:, :cols], row[:, cols:])


def open_kernel(
    x_far, lengths_far, first_gain_far, first_bias_far, key_far, value_far, router_far, q_far,
    o_far, second_gain_far, second_bias_far, return_bias_far, hidden_bias_far, routes_far,
    normed, vecs, keys_ext, key_t, value_n, values_ext, logits, x, q_own, o_own, key_w, value_w,
    router_w, routes, ends_out,
    lengths, first_gain, first_bias, second_gain, second_bias, return_bias, hidden_bias, sems,
):
    spans = [slice(at, at + ROWS) for at in range(0, x.shape[0], ROWS)]
    moves = [(x_far.at[here, :], x.at[here, :]) for here in spans]
    needed = [
        (lengths_far, lengths), (first_gain_far, first_gain), (first_bias_far, first_bias),
        (key_far, key_w), (value_far, value_w), (router_far, router_w),
    ]
    later = [
        (q_far, q_own), (o_far, o_own), (second_gain_far, second_gain),
        (second_bias_far, second_bias), (return_bias_far, return_bias),
        (hidden_bias_far, hidden_bias), (routes_far.at[core_here()], routes),
    ]
    moves = moves[:1] + needed + moves[1:] + later
    copies = [pltpu.make_async_copy(*move, sems.at[j]) for j, move in enumerate(moves)]
    for copy in copies:
        copy.start()
    for copy in copies[: len(needed) + len(spans)]:
        copy.wait()
    head = key_w.shape[0]
    width = x.shape[1]
    ends, end = [], 0
    for slot in range(lengths.shape[1]):
        end = end + lengths[core_here(), slot]
        ends.append(end)
        ends_out[slot : slot + 1, :] = jnp.full((1, ends_out.shape[1]), end, jnp.int32)
    vecs[...] = jnp.zeros_like(vecs)
    for j, vec in enumerate((first_gain, first_bias)):
        vecs[j : j + 1, :] = wide(vec[...]).reshape(1, width)
    pair_w = jnp.concatenate([key_w[...], value_w[...]], axis=0)
    all_w = jnp.concatenate([key_w[...], value_w[...], router_w[...]], axis=0)
    for j, here in enumerate(spans):
        at = j * ROWS
        unit, _ = norm_parts(wide(x[here, :]))
        rows = low(
            unit * vecs[FIRST_GAIN : FIRST_GAIN + 1, :] + vecs[FIRST_BIAS : FIRST_BIAS + 1, :]
        )
        normed[here, :] = rows
        across = dot_nt(all_w, rows)
        key_t[:, here] = low(across[:head, :])
        values_ext[:head, here] = low(across[head : 2 * head, :])
        values_ext[head:, here] = jnp.ones((values_ext.shape[0] - head, ROWS), LOW)
        logits[:, here] = across[2 * head :, :]
        along = low(dot_nt(rows, pair_w))
        places = at + lax.broadcasted_iota(jnp.int32, (ROWS, head), 0)
        lanes = lax.broadcasted_iota(jnp.int32, (ROWS, head), 1)
        marks = low(jnp.where(segment_of(places, ends) == lanes, 1.0, 0.0))
        keys_ext[here, :] = jnp.concatenate([along[:, :head], marks], axis=1)
        value_n[here, :] = jnp.concatenate(
            [along[:, head:], jnp.ones((ROWS, head), LOW)], axis=1
        )
    for copy in copies[len(needed) + len(spans) :]:
        copy.wait()
    for j, vec in enumerate((second_gain, second_bias, return_bias)):
        vecs[SECOND_GAIN + j : SECOND_GAIN + j + 1, :] = wide(vec[...]).reshape(1, width)
    for j in range(hidden_bias.shape[0] // width):
        part = hidden_bias[j * width : (j + 1) * width]
        vecs[HIDDEN_BIAS + j : HIDDEN_BIAS + j + 1, :] = wide(part).reshape(1, width)


def expert_hits(route, experts):
    own = experts // 2
    relative = lax.rem(route - core_here() * own + experts, experts)
    return [relative == e for e in range(experts)]


def forward_kernel(
    normed, x, vecs, q_own, q_other, o_own, o_other, keys_ext, values_ext, logits, routes, ends_in,
    key_t, cot_far, hidden_w_far, return_w_far,
    exps, q_sel, attended, row_facts, placed, middle, hidden_in, hidden_in_t, d_feed, d_feed_t,
    bias_grad, cot, hidden_w, return_w, spread, sems,
):
    moves = ((cot_far, cot), (hidden_w_far, hidden_w), (return_w_far, return_w))
    copies = [pltpu.make_async_copy(*move, sems.at[j]) for j, move in enumerate(moves)]
    for copy in copies:
        copy.start()
    ends = [ends_in[slot, 0] for slot in range(SLOTS)]
    head = q_sel.shape[0]
    tok, half = x.shape[0], q_own.shape[0]
    experts = 2 * half // head
    own = experts // 2
    q_all = [low(dot_nt(q_own[...], normed[...])), low(dot_nt(q_other[...], normed[...]))]
    hits = [expert_hits(routes[m : m + 1, :], experts) for m in range(2)]
    places = lax.broadcasted_iota(jnp.int32, (head, tok), 1)
    subs = lax.broadcasted_iota(jnp.int32, (head, tok), 0)
    fence = low(jnp.where(segment_of(places, ends) == subs, 0.0, MASKED))
    for m in range(2):
        query = jnp.zeros((head, tok), LOW)
        for e in range(experts):
            from_e = q_all[e // own][(e % own) * head : (e % own + 1) * head, :]
            query = jnp.where(hits[m][e], from_e, query)
        lanes = slice(m * tok, (m + 1) * tok)
        q_sel[:, lanes] = query
        spread[:head, lanes] = low(wide(query) * head**-0.5)
        spread[head:, lanes] = fence

    def scores_of(here):
        return dot_nn(keys_ext[...], spread[:, here])

    def attend(here, powers):
        exps[:, here] = powers
        summed = dot_nn(values_ext[...], powers)
        inv = 1.0 / summed[head : head + 1, :]
        attended[:, here] = summed[:head, :] * inv
        row_facts[1:2, here] = inv

    longest_query = jnp.max(jnp.sum(jnp.square(wide(spread[:head, :])), axis=0, keepdims=True))
    longest_key = jnp.max(jnp.sum(jnp.square(wide(key_t[...])), axis=0, keepdims=True))
    within = longest_query * longest_key < REACH * REACH

    @pl.when(within)
    def _():
        for at in range(0, 2 * tok, SPAN):
            here = slice(at, at + SPAN)
            attend(here, low(jnp.exp(scores_of(here))))

    @pl.when(jnp.logical_not(within))
    def _():
        @pl.loop(0, 2 * tok // SPAN)
        def _(turn):
            here = rows_at(turn, SPAN)
            scores = scores_of(here)
            attend(here, low(jnp.exp(scores - jnp.max(scores, axis=0, keepdims=True))))

    ids = lax.broadcasted_iota(jnp.int32, (experts, tok), 0)
    chosen = [
        jnp.sum(jnp.where(ids == routes[m : m + 1, :], logits[...], 0.0), axis=0, keepdims=True)
        for m in range(2)
    ]
    top = jnp.maximum(chosen[0], chosen[1])
    lifts = [jnp.exp(c - top) for c in chosen]
    inv_sum = 1.0 / (lifts[0] + lifts[1])
    gated = []
    for m in range(2):
        lanes = slice(m * tok, (m + 1) * tok)
        gate = lifts[m] * inv_sum
        row_facts[0:1, lanes] = gate
        gated.append(attended[:, lanes] * gate)
    for e in range(experts):
        placed[e * head : (e + 1) * head, :] = low(
            jnp.where(hits[0][e], gated[0], jnp.where(hits[1][e], gated[1], 0.0))
        )
    copies[0].wait()
    total = jnp.zeros(bias_grad.shape, WIDE)
    for at in range(0, tok, SPAN):
        here = slice(at, at + SPAN)
        branch = dot_tn(placed[:half, here], o_own[...]) + dot_tn(placed[half:, here], o_other[...])
        spots = at + lax.broadcasted_iota(jnp.int32, (SPAN, 1), 0)
        mid = wide(x[here, :]) + jnp.where(spots < ends[-1], branch, 0.0)
        middle[here, :] = mid
        unit, _ = norm_parts(mid)
        hidden = (
            unit * vecs[SECOND_GAIN : SECOND_GAIN + 1, :] + vecs[SECOND_BIAS : SECOND_BIAS + 1, :]
        )
        hidden_in[here, :] = low(hidden)
        hidden_in_t[:, here] = low(hidden.T)
        masked = jnp.where(spots < ends[-1], wide(cot[here, :]), 0.0)
        d_feed[here, :] = low(masked)
        d_feed_t[:, here] = low(masked.T)
        total = total + jnp.sum(masked, axis=0, keepdims=True)
    bias_grad[...] = total
    for copy in copies[1:]:
        copy.wait()


def feed_kernel(
    units_of, joint, hidden_in, hidden_in_t, d_feed, d_feed_t, vecs, hidden_w, return_w, *outs
):
    units = units_of()
    grads_all = outs[-1] if joint else None
    for j, unit in enumerate(units):
        act, d_before, bias_grad = outs[3 * j : 3 * j + 3]
        cols = act.shape[1]
        at = rows_at(unit, cols)
        weight_in, weight_out = hidden_w[:, at], return_w[at, :]
        bias = bias_row(vecs, unit, cols)
        bias_sum = jnp.zeros(bias_grad.shape, WIDE)
        for row in range(0, act.shape[0], ROWS):
            here = slice(row, row + ROWS)
            x = dot_nn(hidden_in[here, :], weight_in) + bias
            d_act = dot_nt(d_feed[here, :], weight_out)
            squared = x * x
            rise = 0.5 + 0.5 * jnp.tanh(x * (CURVE + CURVE * CUBIC * squared))
            out = x * rise
            slope = rise + out * (1.0 - rise) * (2 * CURVE + 6 * CURVE * CUBIC * squared)
            act[here, :] = low(out)
            d_x = d_act * slope
            d_before[here, :] = low(d_x)
            bias_sum = bias_sum + jnp.sum(d_x, axis=0, keepdims=True)
        bias_grad[...] = bias_sum
        width = hidden_in.shape[1]
        rows = slice(j * width, (j + 1) * width)
        grads_all[rows, :cols] = low(dot_nn(hidden_in_t[...], d_before[...]))
        grads_all[rows, cols:] = low(dot_nn(d_feed_t[...], act[...]))


def spans_of(units, cols):
    return [rows_at(unit, cols) for unit in units]


def middle_kernel(units_of, *refs):
    d_befores, (hidden_w, vecs, middle, cot, ends_in) = refs[:PARTS], refs[PARTS : PARTS + 5]
    d_middle, d_low, gain_grad, bias_grad = refs[PARTS + 5 :]
    end = ends_in[SLOTS - 1, 0]
    spans = spans_of(units_of(), d_befores[0].shape[1])
    gain = vecs[SECOND_GAIN : SECOND_GAIN + 1, :]
    gain_sum = jnp.zeros(gain_grad.shape, WIDE)
    bias_sum = jnp.zeros(bias_grad.shape, WIDE)
    for at in range(0, middle.shape[0], ROWS):
        here = slice(at, at + ROWS)
        d_hidden = 0.0
        for part, span in zip(d_befores, spans):
            d_hidden = d_hidden + dot_nt(part[here, :], hidden_w[:, span])
        valid = at + lax.broadcasted_iota(jnp.int32, (ROWS, 1), 0) < end
        unit, inv = norm_parts(middle[here, :])
        d_mid = wide(cot[here, :]) + norm_back(d_hidden, unit, inv, gain)
        d_middle[here, :] = d_mid
        d_low[here, :] = low(jnp.where(valid, d_mid, 0.0))
        gain_sum = gain_sum + jnp.sum(d_hidden * unit, axis=0, keepdims=True)
        bias_sum = bias_sum + jnp.sum(d_hidden, axis=0, keepdims=True)
    gain_grad[...] = gain_sum
    bias_grad[...] = bias_sum


def rows_out(near, far, sems, compute):
    blocks = near.shape[0] // ROWS

    def leaving(turn):
        here = rows_at(turn, ROWS)
        return pltpu.make_async_copy(near.at[here, :], far.at[here, :], sems.at[turn])

    @pl.loop(0, blocks)
    def _(turn):
        compute(rows_at(turn, ROWS), turn * ROWS)
        leaving(turn).start()

    for turn in range(blocks):
        leaving(turn).wait()


def layer_kernel(units_of, *refs):
    acts, (return_w, vecs, middle, ends_in) = refs[:PARTS], refs[PARTS : PARTS + 4]
    token, far, near, sems = refs[PARTS + 4 :]
    token[...] = jnp.zeros_like(token)
    end = ends_in[SLOTS - 1, 0]
    spans = spans_of(units_of(), acts[0].shape[1])

    def compute(here, at):
        feed = vecs[RETURN_BIAS : RETURN_BIAS + 1, :]
        for part, span in zip(acts, spans):
            feed = feed + dot_nn(part[here, :], return_w[span, :])
        valid = at + lax.broadcasted_iota(jnp.int32, (ROWS, 1), 0) < end
        near[here, :] = middle[here, :] + jnp.where(valid, feed, 0.0)

    rows_out(near, far, sems, compute)


def attention_back_kernel(
    d_low, exps, q_sel, attended, row_facts, placed, key_t, value_n, o_own, o_other, routes,
    d_stack, grad_o, spread, d_scores, d_queries,
):
    head = key_t.shape[0]
    tok, half = d_low.shape[0], o_own.shape[0]
    experts = 2 * half // head
    own = experts // 2
    scale = head**-0.5
    d_all = [dot_nt(o_own[...], d_low[...]), dot_nt(o_other[...], d_low[...])]
    hits = [expert_hits(routes[m : m + 1, :], experts) for m in range(2)]
    halves = [slice(m * tok, (m + 1) * tok) for m in range(2)]
    gates = [row_facts[0:1, lanes] for lanes in halves]
    subs = lax.broadcasted_iota(jnp.int32, (head, tok), 0)
    d_gates = []
    for m, lanes in enumerate(halves):
        d_raw = jnp.zeros((head, tok), WIDE)
        for e in range(experts):
            from_e = d_all[e // own][(e % own) * head : (e % own + 1) * head, :]
            d_raw = jnp.where(hits[m][e], from_e, d_raw)
        att = attended[:, lanes]
        d_gates.append(jnp.sum(d_raw * att, axis=0, keepdims=True))
        d_att = low(d_raw * (gates[m] * row_facts[1:2, lanes]))
        inner = jnp.sum(wide(d_att) * att, axis=0, keepdims=True)
        inner_high = wide(low(inner))
        tail = jnp.where(subs == 0, -inner_high, jnp.where(subs == 1, inner_high - inner, 0.0))
        spread[:head, lanes] = d_att
        spread[head:, lanes] = low(tail)
    mean_gate = gates[0] * d_gates[0] + gates[1] * d_gates[1]
    ids = lax.broadcasted_iota(jnp.int32, (experts, tok), 0)
    d_logits = sum(
        jnp.where(ids == routes[m : m + 1, :], gates[m] * (d_gates[m] - mean_gate), 0.0)
        for m in range(2)
    )
    high = wide(low(d_logits))
    d_stack[2 * half + 2 * head :, :] = low(jnp.concatenate([high, d_logits - high], axis=0))

    def d_probs_of(at):
        return dot_nn(value_n[...], spread[:, at : at + ROWS])

    d_probs = d_probs_of(0)
    for at in range(0, 2 * tok, ROWS):
        later = d_probs_of(at + ROWS) if at + ROWS < 2 * tok else None
        here = slice(at, at + ROWS)
        d_score = low(wide(exps[:, here]) * d_probs)
        d_scores[:, here] = d_score
        d_queries[:, here] = dot_nn(key_t[...], d_score) * scale
        d_probs = later
    d_values = dot_nt(exps[...], spread[:head, :])
    d_keys = dot_nt(d_scores[...], q_sel[...]) * scale
    d_stack[2 * half : 2 * half + head, :] = low(d_keys.T)
    d_stack[2 * half + head : 2 * half + 2 * head, :] = low(d_values.T)
    first, second = d_queries[:, halves[0]], d_queries[:, halves[1]]
    for e in range(experts):
        d_stack[e * head : (e + 1) * head, :] = low(
            jnp.where(hits[0][e], first, jnp.where(hits[1][e], second, 0.0))
        )
    grad_o[...] = dot_nn(placed[...], d_low[...])


def close_kernel(
    units_of, d_stack, grad_o, q_own, q_other, normed, vecs, return_bias_grad, second_gain_grad,
    second_bias_grad, key_w, value_w, router_w, *rest,
):
    bias_parts, (own_grads, other_grads, common) = rest[:PARTS], rest[PARTS:]
    half, head, experts = q_own.shape[0], key_w.shape[0], router_w.shape[0]
    owned = at_kv = 2 * half
    rows_in = normed[...]
    parts = ((0, half, q_own[...]), (half, at_kv, q_other[...]))
    tail_w = jnp.concatenate([key_w[...], value_w[...], router_w[...], router_w[...]], axis=0)
    parts = parts + ((at_kv, d_stack.shape[0], tail_w),)
    bias_sum, product_sum, grads = 0.0, 0.0, []
    for start, stop, weights in parts:
        stack = d_stack[start:stop, :]
        grad = dot_nn(stack, rows_in)
        grads.append(grad)
        row_sums = jnp.sum(wide(stack), axis=1, keepdims=True)
        bias_sum = bias_sum + jnp.sum(row_sums * wide(weights), axis=0, keepdims=True)
        product_sum = product_sum + jnp.sum(grad * wide(weights), axis=0, keepdims=True)
    gain = vecs[FIRST_GAIN : FIRST_GAIN + 1, :]
    gain_sum = (product_sum - vecs[FIRST_BIAS : FIRST_BIAS + 1, :] * bias_sum) / gain
    own_grads[:half, :] = low(grads[0])
    other_grads[:half, :] = low(grads[1])
    own_grads[half:owned, :] = low(grad_o[:half, :])
    other_grads[half:owned, :] = low(grad_o[half:, :])
    tail = grads[2]
    common[...] = jnp.zeros_like(common)
    common[: 2 * head, :] = tail[: 2 * head, :]
    row = 2 * head
    common[row : row + experts, :] = (
        tail[2 * head : 2 * head + experts, :] + tail[2 * head + experts :, :]
    )
    row = row + experts
    rows = (gain_sum, bias_sum, second_gain_grad[...], second_bias_grad[...], return_bias_grad[...])
    for j, values in enumerate(rows):
        common[row + j : row + j + 1, :] = values
    for unit, part in zip(units_of(), bias_parts):
        cols = part.shape[1]
        at = pl.ds(row + HIDDEN_BIAS + unit // 2, 1)
        there_now = common[at, :]
        doubled = jnp.concatenate([part[...], part[...]], axis=1)
        lanes = lax.broadcasted_iota(jnp.int32, doubled.shape, 1)
        common[at, :] = jnp.where(lanes // cols == unit % 2, doubled, there_now)
    own_grads[owned:, :] = low(common[...])
    other_grads[owned:, :] = low(common[...])


def input_kernel(
    d_stack, q_own, q_other, key_w, value_w, router_w, x, d_middle, vecs,
    token, far, near, sems,
):
    token[...] = jnp.zeros_like(token)
    half = q_own.shape[0]
    at_kv = 2 * half
    tail_w = jnp.concatenate([key_w[...], value_w[...], router_w[...], router_w[...]], axis=0)
    gain = vecs[FIRST_GAIN : FIRST_GAIN + 1, :]

    def compute(here, at):
        d_normed = dot_tn(d_stack[:half, here], q_own[...])
        d_normed = d_normed + dot_tn(d_stack[half:at_kv, here], q_other[...])
        d_normed = d_normed + dot_tn(d_stack[at_kv:, here], tail_w)
        unit, inv = norm_parts(wide(x[here, :]))
        near[here, :] = d_middle[here, :] + norm_back(d_normed, unit, inv, gain)

    rows_out(near, far, sems, compute)


def halvings(n_dp):
    return n_dp.bit_length() - 3


def step_orders(n_dp):
    first = list(range(halvings(n_dp)))
    second = []
    for at in range(0, len(first), 2):
        second += first[at : at + 2][::-1]
    return first, second


def pairs_of(n_dp, step):
    orders = step_orders(n_dp)
    return [
        (chip * 2 + core, (chip ^ (1 << orders[core][step])) * 2 + core)
        for chip in range(n_dp)
        for core in range(2)
    ]


def quad_pairs(n_dp, turn):
    return [
        (chip * 2 + core, (chip ^ (turn << halvings(n_dp))) * 2 + core)
        for chip in range(n_dp)
        for core in range(2)
    ]


def cross_pairs(n_dp, turn):
    low_bit = halvings(n_dp)
    return [
        (chip * 2 + core, (chip ^ (1 << (low_bit + turn))) * 2 + core)
        for chip in range(n_dp)
        for core in range(2)
    ]


def core_swap(values, n_dp):
    return lax.ppermute(values, AXES, [(at, at ^ 1) for at in range(2 * n_dp)])


def bit_here(n_dp, step, core=None):
    first, second = step_orders(n_dp)
    chip = lax.axis_index("dp")
    core = core_here() if core is None else core
    return jnp.where(core == 0, chip >> first[step], chip >> second[step]) & 1


def units_here(n_dp, entries):
    core = core_here()
    mine, theirs = bit_here(n_dp, 0), bit_here(n_dp, 0, 1 - core)
    other = 1 - core
    blocks = [2 * other + 1 - theirs, 2 * core + 1 - mine, 2 * other + theirs, 2 * core + mine]
    return [2 * blocks[entry // 2] + entry % 2 for entry in entries]


def rows_at(index, size):
    return pl.ds(pl.multiple_of(index * size, size), size)


def add_kernel(*refs):
    total = wide(refs[0][...])
    for ref in refs[1:-1]:
        total = total + wide(ref[...])
    refs[-1][...] = low(total)


def rows_of(ref, at, size):
    return wide(ref[pl.ds(pl.multiple_of(at, size), size), :])


def partial_sum(n_dp, terms, step, last_kept):
    start = step - len(terms) + 1
    size = terms[0][0].shape[0] >> (step - start + 1)
    at, total = 0, 0.0
    for j in range(step, start - 1, -1):
        bit = bit_here(n_dp, j)
        bit = bit if last_kept or j < step else 1 - bit
        at = at + bit * (size << (step - j))
        for ref in terms[j - start]:
            total = total + rows_of(ref, at, size)
    return total


def group(refs, counts):
    refs = list(refs)
    return [[refs.pop(0) for _ in range(count)] for count in counts]


def split_terms(terms, joint):
    parts = []
    for part in range(2):
        chosen = []
        for refs, flags in zip(terms, joint):
            chosen.append([])
            for ref, flag in zip(refs, flags):
                half = ref.shape[0] // 2
                if flag == 2:
                    chosen[-1].append(ref.at[pl.ds(part * half, half), :])
                elif flag == part:
                    chosen[-1].append(ref)
        parts.append(chosen)
    return parts


def send_kernel(n_dp, step, counts, joint, *refs):
    out = refs[-1]
    terms = group(refs[:-1], counts)
    if joint is None:
        out[...] = low(partial_sum(n_dp, terms, step, False))
        return
    size = out.shape[0] // 2
    for part, chosen in enumerate(split_terms(terms, joint)):
        out[part * size : (part + 1) * size, :] = low(partial_sum(n_dp, chosen, step, False))


def kept_kernel(n_dp, step, counts, *refs):
    *terms, last = group(refs[:-1], counts)
    refs[-1][...] = low(partial_sum(n_dp, terms, step, True) + wide(last[0][...]))


def spot_here(n_dp, turn):
    return jnp.bitwise_xor(lax.axis_index("dp") >> halvings(n_dp), turn)


def quarters_kernel(n_dp, step, counts, joint, *refs):
    count = sum(counts)
    terms = group(refs[:count], counts)
    outs, total = refs[count:-1], refs[-1]
    size = total.shape[0] // 2
    for part, (*chosen, last) in enumerate(split_terms(terms, joint)):
        total[part * size : (part + 1) * size, :] = partial_sum(
            n_dp, chosen, step, True
        ) + wide(last[0][...])
    cols = outs[0].shape[1]
    for turn, out in enumerate(outs):
        out[...] = low(total[:, rows_at(spot_here(n_dp, turn), cols)])


def row_of_four(n_dp, part, *refs):
    pieces, out = refs[:4], refs[4]
    size, cols = out.shape[0], pieces[0].shape[1]
    for turn, piece in enumerate(pieces):
        at = rows_at(spot_here(n_dp, turn), cols)
        out[:, at] = piece[part * size : (part + 1) * size, :]


def join_kernel(n_dp, step, mine, got, out):
    size = mine.shape[0]
    bit = bit_here(n_dp, step)
    out[rows_at(bit, size), :] = mine[...]
    out[rows_at(1 - bit, size), :] = got[...]


def pass_kernel(source, out):
    out[...] = source[...]


def stack_kernel(first, second, out):
    size = first.shape[0]
    out[:size, :] = first[...]
    out[size:, :] = second[...]


def place_kernel(units_of, count, more, *refs):
    hidden, returned, left, right, sems = refs[-5:]
    copies = []
    width = left.shape[1]
    parts = []
    for ref in refs[:count]:
        parts += [ref.at[pl.ds(row, width), :] for row in range(0, ref.shape[0], width)]
    for j, (unit, part) in enumerate(zip(units_of(), parts)):
        cols = part.shape[1] // 2
        at = rows_at(unit, cols)
        left[j] = wide(part[:, :cols])
        copies.append(pltpu.make_async_copy(left.at[j], hidden.at[:, at], sems.at[2 * j]))
        copies[-1].start()
        right[j] = wide(part[:, cols:]).T
        copies.append(pltpu.make_async_copy(right.at[j], returned.at[at, :], sems.at[2 * j + 1]))
        copies[-1].start()
    if more:
        refs[-6][...] = jnp.zeros_like(refs[-6])
    for copy in copies:
        copy.wait()


def finish_kernel(n_dp, mine, got, token, query_g, output_g, key_g, value_g, router_g, *refs):
    vectors, whole = refs[:-1], refs[-1]
    token[...] = jnp.zeros_like(token)
    size, width = mine.shape
    bit = bit_here(n_dp, 0)
    whole[rows_at(bit, size), :] = wide(mine[...])
    whole[rows_at(1 - bit, size), :] = wide(got[...])
    row = 0
    for out in (query_g, output_g, key_g, value_g, router_g):
        out[...] = whole[row : row + out.shape[0], :]
        row = row + out.shape[0]
    for j, vector in enumerate(vectors[:-1]):
        vector[...] = whole[row + j, :]
    row = row + len(vectors) - 1
    for j in range(vectors[-1].shape[0] // width):
        vectors[-1][j * width : (j + 1) * width] = whole[row + j, :]


def local(
    inputs, cotangent, lengths, routes, first_gain, first_bias, router_weight, key_weight,
    value_weight, query_weight, output_weight, second_gain, second_bias, hidden_weight,
    hidden_bias, return_weight, return_bias,
):
    tok, width = inputs.shape
    ff = hidden_weight.shape[1]
    n_dp = lax.axis_size("dp")
    own, _, head = query_weight.shape
    experts = 2 * own
    half = own * head
    blocks = tok // ROWS

    q_own = jnp.transpose(query_weight, (0, 2, 1)).reshape(half, width)
    o_own = output_weight.reshape(half, width)
    q_other, o_other = core_swap(q_own, n_dp), core_swap(o_own, n_dp)
    vec_rows = 5 + ff // width
    program = Program()
    call = program.call
    (
        normed, vecs, keys_ext, key_t, value_n, values_ext, logits, x, q_own, o_own, key_w, value_w,
        router_w, routes, ends,
    ) = call(
        open_kernel, "first_norm", [],
        [
            held((tok, width), LOW), held((vec_rows + -vec_rows % 8, width), WIDE),
            held((tok, 2 * head), LOW), held((head, tok), LOW), held((tok, 2 * head), LOW),
            held((head + 16, tok), LOW), held((experts, tok), WIDE), held((tok, width), LOW),
            held((half, width), LOW), held((half, width), LOW), held((head, width), LOW),
            held((head, width), LOW), held((experts, width), LOW), held((2, tok), jnp.int32),
            held((8, 128), jnp.int32),
        ],
        scratch=[pltpu.SMEM(lengths.shape[1:], jnp.int32)]
        + [pltpu.VMEM((width,), LOW)] * 5
        + [pltpu.VMEM((ff,), LOW), pltpu.SemaphoreType.DMA((blocks + 13,))],
        far=[
            inputs, lengths[0], first_gain, first_bias, key_weight.T, value_weight.T,
            router_weight.T, q_own, o_own, second_gain, second_bias, return_bias, hidden_bias,
            jnp.transpose(routes[0], (0, 2, 1)),
        ],
    )
    (
        exps, q_sel, attended, row_facts, placed, middle, hidden_in, hidden_in_t, d_feed, d_feed_t,
        return_bias_grad, cot, hidden_w, return_w,
    ) = call(
        forward_kernel, "attention_forward",
        [
            normed, x, vecs, q_own, q_other, o_own, o_other, keys_ext, values_ext, logits, routes,
            ends, key_t,
        ],
        [
            held((tok, 2 * tok), LOW), held((head, 2 * tok), LOW), held((head, 2 * tok), WIDE),
            held((8, 2 * tok), WIDE), held((2 * half, tok), LOW), held((tok, width), WIDE),
            held((tok, width), LOW), held((width, tok), LOW), held((tok, width), LOW),
            held((width, tok), LOW), held((1, width), WIDE), held((tok, width), LOW),
            held(hidden_weight.shape, LOW), held(return_weight.shape, LOW),
        ],
        scratch=[pltpu.VMEM((2 * head, 2 * tok), LOW), pltpu.SemaphoreType.DMA((3,))],
        far=[cotangent, hidden_weight, return_weight],
    )

    cols = ff // PARTS
    units = lambda *entries: functools.partial(units_here, n_dp, entries)
    steps = halvings(n_dp)

    def feed(*entries):
        outs = call(
            functools.partial(feed_kernel, units(*entries), True), f"feed_{entries[0]}",
            [hidden_in, hidden_in_t, d_feed, d_feed_t, vecs, hidden_w, return_w],
            [held((tok, cols), LOW), held((tok, cols), LOW), held((1, cols), WIDE)] * len(entries)
            + [there((len(entries) * width, 2 * cols), LOW)],
        )
        return list(zip(*[iter(outs[:-1])] * 3)), outs[-1]

    def add(name, *terms):
        return call(add_kernel, name, terms, there(terms[0].shape, LOW))

    parts_a, theirs = feed(0)
    swapped = core_swap(theirs, n_dp)
    parts_c, mine = feed(2)
    sent_a = lax.ppermute(add("feed_add_0", mine, swapped), AXES, pairs_of(n_dp, 0))
    parts_b, theirs = feed(1)
    swapped = core_swap(theirs, n_dp)
    parts_d, mine = feed(3)
    sent_b = lax.ppermute(add("feed_add_1", mine, swapped), AXES, pairs_of(n_dp, 0))
    parts_e, theirs = feed(4, 5)
    swapped = core_swap(theirs, n_dp)
    parts_f, mine = feed(6, 7)
    parts = parts_a + parts_b + parts_c + parts_d + parts_e + parts_f

    every = units(*range(PARTS))
    d_middle, d_low, second_gain_grad, second_bias_grad = call(
        functools.partial(middle_kernel, every), "second_norm_back",
        [p[1] for p in parts] + [hidden_w, vecs, middle, cot, ends],
        [
            held((tok, width), WIDE), held((tok, width), LOW), held((1, width), WIDE),
            held((1, width), WIDE),
        ],
    )

    feed_terms, feed_joint = [[sent_a, sent_b, swapped, mine]], [[0, 1, 2, 2]]

    def feed_send(step):
        counts = [len(t) for t in feed_terms]
        part = call(
            functools.partial(send_kernel, n_dp, step, counts, list(feed_joint)),
            f"feed_send_{step}", sum(feed_terms, []), there((2 * width >> step, 2 * cols), LOW),
        )
        feed_terms.append([lax.ppermute(part, AXES, pairs_of(n_dp, step))])
        feed_joint.append([2])

    for step in range(1, steps):
        feed_send(step)
    d_stack, grad_o = call(
        attention_back_kernel, "attention_backward",
        [d_low, exps, q_sel, attended, row_facts, placed, key_t, value_n, o_own, o_other, routes],
        [held((2 * half + 2 * head + 2 * experts, tok), LOW), held((2 * half, width), WIDE)],
        scratch=[
            pltpu.VMEM((2 * head, 2 * tok), LOW), pltpu.VMEM((tok, 2 * tok), LOW),
            pltpu.VMEM((head, 2 * tok), WIDE),
        ],
    )
    shared = 2 * head + experts + 5 + ff // width
    shared = shared + -(2 * half + shared) % (16 << steps)
    rows = 2 * half + shared
    own_grads, other_grads = call(
        functools.partial(close_kernel, every), "projection_grads",
        [
            d_stack, grad_o, q_own, q_other, normed, vecs, return_bias_grad, second_gain_grad,
            second_bias_grad, key_w, value_w, router_w, *[p[2] for p in parts],
        ],
        [there((rows, width), LOW), there((rows, width), LOW)],
        scratch=[pltpu.VMEM((shared, width), WIDE)],
    )

    def output(kernel, name, operands):
        _, out = call(
            kernel, name, operands, [held((8, 128), WIDE), there((tok, width), WIDE)],
            scratch=[pltpu.VMEM((tok, width), WIDE), pltpu.SemaphoreType.DMA((blocks,))],
            far_out=1,
        )
        return out

    rest_terms = [[own_grads, core_swap(other_grads, n_dp)]]
    counts = [len(t) for t in feed_terms]
    own_piece, *pieces = call(
        functools.partial(quarters_kernel, n_dp, steps - 1, counts, feed_joint), "feed_cut",
        sum(feed_terms, []), [there((2 * width >> (steps - 1), cols // 2), LOW)] * 4,
        scratch=[pltpu.VMEM((2 * width >> (steps - 1), 2 * cols), WIDE)],
    )

    def across(values):
        return [
            lax.ppermute(v, AXES, quad_pairs(n_dp, t + 1)) for t, v in enumerate(values)
        ]

    pieces = across(pieces)


    def rest_send(step):
        counts = [len(t) for t in rest_terms]
        part = call(
            functools.partial(send_kernel, n_dp, step, counts, None), f"rest_send_{step}",
            sum(rest_terms, []), there((rows >> (step + 1), width), LOW),
        )
        rest_terms.append([lax.ppermute(part, AXES, pairs_of(n_dp, step))])

    def join(name, step, mine, got):
        size, wide_cols = mine.shape
        kernel = functools.partial(join_kernel, n_dp, step)
        joined = call(kernel, name, [mine, got], there((2 * size, wide_cols), LOW))
        return joined, lax.ppermute(joined, AXES, pairs_of(n_dp, step - 1))

    written = None

    def place(name, entries, values, more=True):
        nonlocal written
        count = len(values)
        *_, one, two = call(
            functools.partial(place_kernel, units(*entries), count, more), name, values,
            [held((8, 128), WIDE)] * more + [there((width, ff), WIDE), there((ff, width), WIDE)],
            scratch=[
                pltpu.VMEM((len(entries), width, cols), WIDE),
                pltpu.VMEM((len(entries), cols, width), WIDE),
                pltpu.SemaphoreType.DMA((2 * len(entries),)),
            ],
            far=[] if written is None else written,
            far_out=2,
            aliases=[] if written is None else [(0, 0), (1, 1)],
        )
        written = [one, two]

    rest_send(0)
    layer_out = output(
        functools.partial(layer_kernel, every), "layer_out",
        [p[0] for p in parts] + [return_w, vecs, middle, ends],
    )
    for step in range(1, steps):
        rest_send(step)
    own_piece = add("feed_sum", own_piece, *pieces)
    pieces = across([own_piece] * 3)
    counts = [len(t) for t in rest_terms]
    rest = call(
        functools.partial(kept_kernel, n_dp, steps - 1, counts), "rest_sum", sum(rest_terms, []),
        there((rows >> steps, width), LOW),
    )
    rest_got = lax.ppermute(rest, AXES, cross_pairs(n_dp, 0))
    input_grad = output(
        input_kernel, "first_norm_back",
        [d_stack, q_own, q_other, key_w, value_w, router_w, x, d_middle, vecs],
    )
    size = own_piece.shape[0] // 2
    joined, got = [None] * 2, [None] * 2
    for part in range(2):
        joined[part] = call(
            functools.partial(row_of_four, n_dp, part), f"feed_row_{part}", [own_piece] + pieces,
            there((size, 2 * cols), LOW),
        )
        got[part] = lax.ppermute(joined[part], AXES, pairs_of(n_dp, steps - 1))
    rest = add("rest_add_0", rest, rest_got)
    rest_got = lax.ppermute(rest, AXES, cross_pairs(n_dp, 1))
    for step in reversed(range(1, steps)):
        for part in range(2):
            name = f"feed_join_{step}_{part}"
            joined[part], got[part] = join(name, step, joined[part], got[part])
            if step == 1:
                place(f"place_own_{part}", (6 + part,), [joined[part]])
    both = call(stack_kernel, "feed_own", joined, there((2 * width, 2 * cols), LOW))
    other = core_swap(both, n_dp)
    rest = add("rest_add_1", rest, rest_got)
    rest_got = lax.ppermute(rest, AXES, pairs_of(n_dp, steps - 1))
    place("place_other", (4, 5), [other])
    far = []

    def place_got(part):
        row = call(pass_kernel, f"feed_got_{part}", [got[part]], there((width, 2 * cols), LOW))
        far.append(core_swap(row, n_dp))
        place(f"place_got_{part}", (2 + part,), [row])

    place_got(0)
    for step in reversed(range(1, steps)):
        rest, rest_got = join(f"rest_join_{step}", step, rest, rest_got)
    place_got(1)
    place("place_far", (0, 1), far)
    vectors = [there((width,), WIDE)] * 5 + [there((ff,), WIDE)]
    _, query_grad, output_grad, key_g, value_g, router_g, fg, fb, sg, sb, rb, hb = call(
        functools.partial(finish_kernel, n_dp), "finish", [rest, rest_got],
        [held((8, 128), WIDE)] + [there((half, width), WIDE)] * 2 + [there((head, width), WIDE)] * 2
        + [there((experts, width), WIDE)] + vectors,
        scratch=[pltpu.VMEM((rows, width), WIDE)],
    )
    hidden_grad, return_grad = written
    return (
        layer_out,
        input_grad,
        fg,
        fb,
        router_g.T,
        key_g.T,
        value_g.T,
        jnp.transpose(query_grad.reshape(-1, head, width), (0, 2, 1)),
        output_grad.reshape(-1, head, width),
        sg,
        sb,
        hidden_grad,
        hb,
        return_grad,
        rb,
    )


def solution(mesh):
    rows = P(AXES, None)
    cut = P("expert", None, None)
    in_specs = (
        (rows, rows, P("dp", None, None), P("dp", None, None, None))
        + (P(),) * 5
        + (cut, cut)
        + (P(),) * 6
    )
    out_specs = (rows, rows) + (P(),) * 5 + (cut, cut) + (P(),) * 6
    return jax.shard_map(local, mesh=mesh, in_specs=in_specs, out_specs=out_specs, check_vma=False)
```

profile of v0, /device:TPU:0, one launch (start us, length us, event | category | flops | bytes accessed | tf_op | source)
XLA Modules:
  0.0 98.9 jit_solution(11360493062066244119)
XLA Ops:
  1.2 3.0 %first_norm.1 = (bf16[1024,512]{1,0:T(8,128)(2,1)S(1)}, f32[16,512]{1,0:T(8,128)S(1)}, bf16[1024,128]{1,0:T(8,128)(2,1)S(1)}, bf16[64,1024]{1,0:T(8,128)(2,1)S(1...) custom-call(bf16[1024,512]{1,0:T(8,128)(2,1)} %refs_0_.1, ...), custom_call_target="tpu_custom_call" | custom-call | flops 10000000000 | bytes 1 | tf_op jit(solution)/shard_map/first_norm/pallas_call | solution.py:99
  4.2 5.5 %attention_forward.1 = (bf16[1024,2048]{1,0:T(8,128)(2,1)S(1)}, bf16[64,2048]{1,0:T(8,128)(2,1)S(1)}, f32[64,2048]{1,0:T(8,128)S(1)}, f32[8,2048]{1,0:T(8,128)S(...) custom-call(bf16[1024,512]{1,0:T(8,128)(2,1)S(1)} %get-tuple-element, ...), custom_call_target="tpu_custom_call" | custom-call | flops 10000000000 | bytes 1 | tf_op jit(solution)/shard_map/attention_forward/pallas_call | solution.py:99
  9.7 1.5 %feed_0.1 = (bf16[1024,256]{1,0:T(8,128)(2,1)S(1)}, bf16[1024,256]{1,0:T(8,128)(2,1)S(1)}, f32[1,256]{1,0:T(1,128)S(1)}, bf16[512,512]{1,0:T(8,128)(2,1)S(1)}) custom-call(bf16[1024,512]{1,0:T(8,128)(2,1)S(1)} %get-tuple-element.130.refs_0_, bf16[512,1024]{1,0:T(8,128)(2,1)S(1)} %get-tuple-element.131.refs_1_, ...), custom_call_target="tpu_custom_call" | custom-call | flops 10000000000 | bytes 1 | tf_op jit(solution)/shard_map/feed_0/pallas_call | solution.py:99
  11.7 1.5 %feed_2.1 = (bf16[1024,256]{1,0:T(8,128)(2,1)S(1)}, bf16[1024,256]{1,0:T(8,128)(2,1)S(1)}, f32[1,256]{1,0:T(1,128)S(1)}, bf16[512,512]{1,0:T(8,128)(2,1)S(1)}) custom-call(bf16[1024,512]{1,0:T(8,128)(2,1)S(1)} %get-tuple-element.130.refs_0_, bf16[512,1024]{1,0:T(8,128)(2,1)S(1)} %get-tuple-element.131.refs_1_, ...), custom_call_target="tpu_custom_call" | custom-call | flops 10000000000 | bytes 1 | tf_op jit(solution)/shard_map/feed_2/pallas_call | solution.py:99
  13.4 2.9 %collective-permute-start.4 = (bf16[512,512]{1,0:T(8,128)(2,1)S(1)}, bf16[512,512]{1,0:T(8,128)(2,1)S(1)}, u32[]{:S(2)}, u32[]{:S(2)}) collective-permute-start(bf16[512,512]{1,0:T(8,128)(2,1)S(1)} %feed_add_0.1.refs_7_), channel_id=1, source_target_pairs={{0,2},{1,5},{2,0},{3,7},{4,6},{5,1},{6,4},{7,3},{8,10},{9,13},{10,... | collective-permute-start | bytes 1572872 | tf_op jit(solution)/shard_map/ppermute | solution.py:798
  16.3 1.5 %feed_1.1 = (bf16[1024,256]{1,0:T(8,128)(2,1)S(1)}, bf16[1024,256]{1,0:T(8,128)(2,1)S(1)}, f32[1,256]{1,0:T(1,128)S(1)}, bf16[512,512]{1,0:T(8,128)(2,1)S(1)}) custom-call(bf16[1024,512]{1,0:T(8,128)(2,1)S(1)} %get-tuple-element.130.refs_0_, bf16[512,1024]{1,0:T(8,128)(2,1)S(1)} %get-tuple-element.131.refs_1_, ...), custom_call_target="tpu_custom_call" | custom-call | flops 10000000000 | bytes 1 | tf_op jit(solution)/shard_map/feed_1/pallas_call | solution.py:99
  17.9 1.5 %feed_3.1 = (bf16[1024,256]{1,0:T(8,128)(2,1)S(1)}, bf16[1024,256]{1,0:T(8,128)(2,1)S(1)}, f32[1,256]{1,0:T(1,128)S(1)}, bf16[512,512]{1,0:T(8,128)(2,1)S(1)}) custom-call(bf16[1024,512]{1,0:T(8,128)(2,1)S(1)} %get-tuple-element.130.refs_0_, bf16[512,1024]{1,0:T(8,128)(2,1)S(1)} %get-tuple-element.131.refs_1_, ...), custom_call_target="tpu_custom_call" | custom-call | flops 10000000000 | bytes 1 | tf_op jit(solution)/shard_map/feed_3/pallas_call | solution.py:99
  19.9 1.1 %collective-permute-start.5 = (bf16[512,512]{1,0:T(8,128)(2,1)S(1)}, bf16[512,512]{1,0:T(8,128)(2,1)S(1)}, u32[]{:S(2)}, u32[]{:S(2)}) collective-permute-start(bf16[512,512]{1,0:T(8,128)(2,1)S(1)} %feed_add_1.1.refs_7_), channel_id=1, source_target_pairs={{0,2},{1,5},{2,0},{3,7},{4,6},{5,1},{6,4},{7,3},{8,10},{9,13},{10,... | collective-permute-start | bytes 1572872 | tf_op jit(solution)/shard_map/ppermute | solution.py:802
  21.0 2.8 %feed_4.1 = (bf16[1024,256]{1,0:T(8,128)(2,1)S(1)}, bf16[1024,256]{1,0:T(8,128)(2,1)S(1)}, f32[1,256]{1,0:T(1,128)S(1)}, bf16[1024,256]{1,0:T(8,128)(2,1)S(1)}, ...) custom-call(bf16[1024,512]{1,0:T(8,128)(2,1)S(1)} %get-tuple-element.130.refs_0_, ...), custom_call_target="tpu_custom_call" | custom-call | flops 10000000000 | bytes 1 | tf_op jit(solution)/shard_map/feed_4/pallas_call | solution.py:99
  24.2 3.0 %feed_6.1 = (bf16[1024,256]{1,0:T(8,128)(2,1)S(1)}, bf16[1024,256]{1,0:T(8,128)(2,1)S(1)}, f32[1,256]{1,0:T(1,128)S(1)}, bf16[1024,256]{1,0:T(8,128)(2,1)S(1)}, ...) custom-call(bf16[1024,512]{1,0:T(8,128)(2,1)S(1)} %get-tuple-element.130.refs_0_, ...), custom_call_target="tpu_custom_call" | custom-call | flops 10000000000 | bytes 1 | tf_op jit(solution)/shard_map/feed_6/pallas_call | solution.py:99
  27.2 3.5 %second_norm_back.1 = (f32[1024,512]{1,0:T(8,128)S(1)}, bf16[1024,512]{1,0:T(8,128)(2,1)S(1)}, f32[1,512]{1,0:T(1,128)S(1)}, f32[1,512]{1,0:T(1,128)S(1)}) custom-call(bf16[1024,256]{1,0:T(8,128)(2,1)S(1)} %get-tuple-element.150.refs_0_, bf16[1024,256]{1,0:T(8,128)(2,1)S(1)} %get-tuple-element.151.refs_1_, bf16[1024,256]{1,0:T(8,128)(2,1)S(1)} %get-tuple-element.152.refs_2_, ...), custom_call_target="tpu_custom_call" | custom-call | flops 10000000000 | bytes 1 | tf_op jit(solution)/shard_map/second_norm_back/pallas_call | solution.py:99
  30.9 0.8 collective-permute-start.8
  31.7 5.7 %attention_backward.1 = (bf16[656,1024]{1,0:T(8,128)(2,1)S(1)}, f32[512,512]{1,0:T(8,128)S(1)}) custom-call(bf16[1024,512]{1,0:T(8,128)(2,1)S(1)} %get-tuple-element.159.refs_0_, bf16[1024,2048]{1,0:T(8,128)(2,1)S(1)} %get-tuple-element.136.refs_7_.refs_1_, bf16[64,2048]{1,0:T(8,128)(2,1)S(1)} %get-tuple-element.160.refs_2_, ...), custom_call_target="tpu_custom_call" | custom-call | flops 10000000000 | bytes 1 | tf_op jit(solution)/shard_map/attention_backward/pallas_call | solution.py:99
  37.4 1.2 %projection_grads.1 = (bf16[704,512]{1,0:T(8,128)(2,1)S(1)}, bf16[704,512]{1,0:T(8,128)(2,1)S(1)}) custom-call(bf16[656,1024]{1,0:T(8,128)(2,1)S(1)} %get-tuple-element.168.refs_0_.refs_20_, f32[512,512]{1,0:T(8,128)S(1)} %get-tuple-element.169.refs_1_, bf16[256,512]{1,0:T(8,128)(2,1)S(1)} %get-tuple-element.122.refs_3_.refs_2_.refs_1_, ...), custom_call_target="tpu_custom_call" | custom-call | flops 10000000000 | bytes 1 | tf_op jit(solution)/shard_map/projection_grads/pallas_call | solution.py:99
  38.9 1.3 %collective-permute-done.8.refs_4_ = bf16[512,512]{1,0:T(8,128)(2,1)S(1)} collective-permute-done((bf16[512,512]{1,0:T(8,128)(2,1)S(1)}, bf16[512,512]{1,0:T(8,128)(2,1)S(1)}, u32[]{:S(2)}, u32[]{:S(2)}) %collective-permute-start.8) | collective-permute-done | bytes 524320 | tf_op jit(solution)/shard_map/ppermute | solution.py:826
  40.7 1.6 %collective-permute-start.11 = (bf16[512,128]{1,0:T(8,128)(2,1)S(1)}, bf16[512,128]{1,0:T(8,128)(2,1)S(1)}, u32[]{:S(2)}, u32[]{:S(2)}) collective-permute-start(bf16[512,128]{1,0:T(8,128)(2,1)S(1)} %get-tuple-element.189), channel_id=1, source_target_pairs={{0,8},{1,9},{2,10},{3,11},{4,12},{5,13},{6,14},{7,15},{8,0},{9,1},... | collective-permute-start | bytes 393224 | tf_op jit(solution)/shard_map/ppermute | solution.py:871
  42.3 2.6 %collective-permute-start.12 = (bf16[512,128]{1,0:T(8,128)(2,1)S(1)}, bf16[512,128]{1,0:T(8,128)(2,1)S(1)}, u32[]{:S(2)}, u32[]{:S(2)}) collective-permute-start(bf16[512,128]{1,0:T(8,128)(2,1)S(1)} %get-tuple-element.190), channel_id=1, source_target_pairs={{0,16},{1,17},{2,18},{3,19},{4,20},{5,21},{6,22},{7,23},{8,24},{9,... | collective-permute-start | bytes 393224 | tf_op jit(solution)/shard_map/ppermute | solution.py:871
  45.2 0.7 collective-permute-start.9
  45.9 4.0 %layer_out.1 = (f32[8,128]{1,0:T(8,128)S(1)}, f32[1024,512]{1,0:T(8,128)}) custom-call(bf16[1024,256]{1,0:T(8,128)(2,1)S(1)} %get-tuple-element.137.refs_7_.refs_0_, bf16[1024,256]{1,0:T(8,128)(2,1)S(1)} %get-tuple-element.141.refs_7_.refs_1_, bf16[1024,256]{1,0:T(8,128)(2,1)S(1)} %get-tuple-element.140.refs_2_, ...), custom_call_target="tpu_custom_call" | custom-call | flops 10000000000 | bytes 1 | tf_op jit(solution)/shard_map/layer_out/pallas_call | solution.py:99
  49.9 2.8 %collective-permute-done.9.refs_2_ = bf16[352,512]{1,0:T(8,128)(2,1)S(1)} collective-permute-done((bf16[352,512]{1,0:T(8,128)(2,1)S(1)}, bf16[352,512]{1,0:T(8,128)(2,1)S(1)}, u32[]{:S(2)}, u32[]{:S(2)}) %collective-permute-start.9) | collective-permute-done | bytes 360480 | tf_op jit(solution)/shard_map/ppermute | solution.py:883
  52.8 0.8 collective-permute-start.10
  53.6 1.1 %collective-permute-done.12.refs_2_ = bf16[512,128]{1,0:T(8,128)(2,1)S(1)} collective-permute-done((bf16[512,128]{1,0:T(8,128)(2,1)S(1)}, bf16[512,128]{1,0:T(8,128)(2,1)S(1)}, u32[]{:S(2)}, u32[]{:S(2)}) %collective-permute-start.12) | collective-permute-done | bytes 131104 | tf_op jit(solution)/shard_map/ppermute | solution.py:871
  54.8 2.5 %collective-permute-start.17 = (bf16[512,128]{1,0:T(8,128)(2,1)S(1)}, bf16[512,128]{1,0:T(8,128)(2,1)S(1)}, u32[]{:S(2)}, u32[]{:S(2)}) collective-permute-start(bf16[512,128]{1,0:T(8,128)(2,1)S(1)} %feed_sum.1.refs_4_.refs_0_), channel_id=1, source_target_pairs={{0,24},{1,25},{2,26},{3,27},{4,28},{5,29},{6,30},{7,31},{8,16},{9,... | collective-permute-start | bytes 393224 | tf_op jit(solution)/shard_map/ppermute | solution.py:871
  57.3 1.0 collective-permute-start.16
  58.3 1.0 collective-permute-start.15
  59.4 1.1 %collective-permute-start.14 = (bf16[176,512]{1,0:T(8,128)(2,1)S(1)}, bf16[176,512]{1,0:T(8,128)(2,1)S(1)}, u32[]{:S(2)}, u32[]{:S(2)}) collective-permute-start(bf16[176,512]{1,0:T(8,128)(2,1)S(1)} %rest_sum.1.refs_9_.refs_0_), channel_id=1, source_target_pairs={{0,8},{1,9},{2,10},{3,11},{4,12},{5,13},{6,14},{7,15},{8,0},{9,1},... | collective-permute-start | bytes 540680 | tf_op jit(solution)/shard_map/ppermute | solution.py:924
  60.5 3.1 %first_norm_back.1 = (f32[8,128]{1,0:T(8,128)S(1)}, f32[1024,512]{1,0:T(8,128)}) custom-call(bf16[656,1024]{1,0:T(8,128)(2,1)S(1)} %get-tuple-element.168.refs_0_.refs_20_, bf16[256,512]{1,0:T(8,128)(2,1)S(1)} %get-tuple-element.122.refs_3_.refs_2_.refs_1_, bf16[256,512]{1,0:T(8,128)(2,1)S(1)} %collective-permute-done.refs_4_.refs_3_.refs_2_, ...), custom_call_target="tpu_custom_call" | custom-call | flops 10000000000 | bytes 1 | tf_op jit(solution)/shard_map/first_norm_back/pallas_call | solution.py:99
  63.6 3.8 %collective-permute-done.16.refs_2_ = bf16[512,128]{1,0:T(8,128)(2,1)S(1)} collective-permute-done((bf16[512,128]{1,0:T(8,128)(2,1)S(1)}, bf16[512,128]{1,0:T(8,128)(2,1)S(1)}, u32[]{:S(2)}, u32[]{:S(2)}) %collective-permute-start.16) | collective-permute-done | bytes 131104 | tf_op jit(solution)/shard_map/ppermute | solution.py:871
  67.5 1.5 %collective-permute-start.19 = (bf16[256,512]{1,0:T(8,128)(2,1)S(1)}, bf16[256,512]{1,0:T(8,128)(2,1)S(1)}, u32[]{:S(2)}, u32[]{:S(2)}) collective-permute-start(bf16[256,512]{1,0:T(8,128)(2,1)S(1)} %feed_row_0.1.refs_4_.refs_0_), channel_id=1, source_target_pairs={{0,4},{1,3},{2,6},{3,1},{4,0},{5,7},{6,2},{7,5},{8,12},{9,11},{10,... | collective-permute-start | bytes 786440 | tf_op jit(solution)/shard_map/ppermute | solution.py:936
  69.1 0.7 collective-permute-start.20
  69.8 1.5 %collective-permute-start.18 = (bf16[176,512]{1,0:T(8,128)(2,1)S(1)}, bf16[176,512]{1,0:T(8,128)(2,1)S(1)}, u32[]{:S(2)}, u32[]{:S(2)}) collective-permute-start(bf16[176,512]{1,0:T(8,128)(2,1)S(1)} %rest_add_0.1.refs_2_.refs_0_), channel_id=1, source_target_pairs={{0,16},{1,17},{2,18},{3,19},{4,20},{5,21},{6,22},{7,23},{8,24},{9,... | collective-permute-start | bytes 540680 | tf_op jit(solution)/shard_map/ppermute | solution.py:938
  71.3 3.1 %collective-permute-done.19.refs_1_ = bf16[256,512]{1,0:T(8,128)(2,1)S(1)} collective-permute-done((bf16[256,512]{1,0:T(8,128)(2,1)S(1)}, bf16[256,512]{1,0:T(8,128)(2,1)S(1)}, u32[]{:S(2)}, u32[]{:S(2)}) %collective-permute-start.19) | collective-permute-done | bytes 262176 | tf_op jit(solution)/shard_map/ppermute | solution.py:936
  74.5 1.8 %collective-permute-start.22 = (bf16[512,512]{1,0:T(8,128)(2,1)S(1)}, bf16[512,512]{1,0:T(8,128)(2,1)S(1)}, u32[]{:S(2)}, u32[]{:S(2)}) collective-permute-start(bf16[512,512]{1,0:T(8,128)(2,1)S(1)} %feed_join_1_0.1.refs_0_.refs_1_), channel_id=1, source_target_pairs={{0,2},{1,5},{2,0},{3,7},{4,6},{5,1},{6,4},{7,3},{8,10},{9,13},{10,... | collective-permute-start | bytes 1572872 | tf_op jit(solution)/shard_map/ppermute | solution.py:889
  76.2 1.1 %place_own_0.1 = (f32[8,128]{1,0:T(8,128)S(1)}, f32[512,2048]{1,0:T(8,128)}, f32[2048,512]{1,0:T(8,128)}) custom-call(bf16[512,512]{1,0:T(8,128)(2,1)S(1)} %feed_join_1_0.1.refs_0_.refs_1_, bf16[512,512]{1,0:T(8,128)(2,1)S(1)} %feed_join_1_0.1.refs_0_.refs_1_), custom_call_target="tpu_custom_call" | custom-call | flops 10000000000 | bytes 1 | tf_op jit(solution)/shard_map/place_own_0/pallas_call | solution.py:99
  77.3 2.7 %collective-permute-done.20.refs_1_ = bf16[256,512]{1,0:T(8,128)(2,1)S(1)} collective-permute-done((bf16[256,512]{1,0:T(8,128)(2,1)S(1)}, bf16[256,512]{1,0:T(8,128)(2,1)S(1)}, u32[]{:S(2)}, u32[]{:S(2)}) %collective-permute-start.20) | collective-permute-done | bytes 262176 | tf_op jit(solution)/shard_map/ppermute | solution.py:936
  80.1 1.8 %collective-permute-start.26 = (bf16[512,512]{1,0:T(8,128)(2,1)S(1)}, bf16[512,512]{1,0:T(8,128)(2,1)S(1)}, u32[]{:S(2)}, u32[]{:S(2)}) collective-permute-start(bf16[512,512]{1,0:T(8,128)(2,1)S(1)} %feed_join_1_1.1.refs_0_.refs_3_.refs_1_), channel_id=1, source_target_pairs={{0,2},{1,5},{2,0},{3,7},{4,6},{5,1},{6,4},{7,3},{8,10},{9,13},{10,... | collective-permute-start | bytes 1572872 | tf_op jit(solution)/shard_map/ppermute | solution.py:889
  81.9 1.1 %place_own_1.1 = (f32[8,128]{1,0:T(8,128)S(1)}, f32[512,2048]{1,0:T(8,128)}, f32[2048,512]{1,0:T(8,128)}) custom-call(bf16[512,512]{1,0:T(8,128)(2,1)S(1)} %feed_join_1_1.1.refs_0_.refs_3_.refs_1_, f32[512,2048]{1,0:T(8,128)} %get-tuple-element.195.refs_1_, f32[2048,512]{1,0:T(8,128)} %get-tuple-element.196.refs_2_, ...), custom_call_target="tpu_custom_call", output_to_operand_aliasing={{1}: (1, {}), {2}: (2, {})} | custom-call | flops 10000000000 | bytes 1 | tf_op jit(solution)/shard_map/place_own_1/pallas_call | solution.py:99
  83.2 1.7 %collective-permute-start.21 = (bf16[176,512]{1,0:T(8,128)(2,1)S(1)}, bf16[176,512]{1,0:T(8,128)(2,1)S(1)}, u32[]{:S(2)}, u32[]{:S(2)}) collective-permute-start(bf16[176,512]{1,0:T(8,128)(2,1)S(1)} %rest_add_1.1.refs_3_.refs_0_), channel_id=1, source_target_pairs={{0,4},{1,3},{2,6},{3,1},{4,0},{5,7},{6,2},{7,5},{8,12},{9,11},{10,... | collective-permute-start | bytes 540680 | tf_op jit(solution)/shard_map/ppermute | solution.py:948
  84.9 0.9 collective-permute-done.23.refs_0_
  85.8 1.5 %place_other.1 = (f32[8,128]{1,0:T(8,128)S(1)}, f32[512,2048]{1,0:T(8,128)}, f32[2048,512]{1,0:T(8,128)}) custom-call(bf16[1024,512]{1,0:T(8,128)(2,1)S(1)} %collective-permute-done.23.refs_0_, f32[512,2048]{1,0:T(8,128)} %get-tuple-element.198.refs_1_, f32[2048,512]{1,0:T(8,128)} %get-tuple-element.199.refs_2_, ...), custom_call_target="tpu_custom_call", output_to_operand_aliasing={{1}: (1, {}), {2}: (2, {})} | custom-call | flops 10000000000 | bytes 1 | tf_op jit(solution)/shard_map/place_other/pallas_call | solution.py:99
  87.5 1.1 %place_got_0.1 = (f32[8,128]{1,0:T(8,128)S(1)}, f32[512,2048]{1,0:T(8,128)}, f32[2048,512]{1,0:T(8,128)}) custom-call(bf16[512,512]{1,0:T(8,128)(2,1)S(1)} %feed_got_0.1.refs_0_.refs_3_, f32[512,2048]{1,0:T(8,128)} %get-tuple-element.201.refs_1_, f32[2048,512]{1,0:T(8,128)} %get-tuple-element.202.refs_2_, ...), custom_call_target="tpu_custom_call", output_to_operand_aliasing={{1}: (1, {}), {2}: (2, {})} | custom-call | flops 10000000000 | bytes 1 | tf_op jit(solution)/shard_map/place_got_0/pallas_call | solution.py:99
  88.6 1.4 %collective-permute-done.21.refs_1_ = bf16[176,512]{1,0:T(8,128)(2,1)S(1)} collective-permute-done((bf16[176,512]{1,0:T(8,128)(2,1)S(1)}, bf16[176,512]{1,0:T(8,128)(2,1)S(1)}, u32[]{:S(2)}, u32[]{:S(2)}) %collective-permute-start.21) | collective-permute-done | bytes 180256 | tf_op jit(solution)/shard_map/ppermute | solution.py:948
  90.0 1.2 %collective-permute-start.24 = (bf16[352,512]{1,0:T(8,128)(2,1)S(1)}, bf16[352,512]{1,0:T(8,128)(2,1)S(1)}, u32[]{:S(2)}, u32[]{:S(2)}) collective-permute-start(bf16[352,512]{1,0:T(8,128)(2,1)S(1)} %rest_join_1.1.refs_1_.refs_0_), channel_id=1, source_target_pairs={{0,2},{1,5},{2,0},{3,7},{4,6},{5,1},{6,4},{7,3},{8,10},{9,13},{10,... | collective-permute-start | bytes 1081352 | tf_op jit(solution)/shard_map/ppermute | solution.py:889
  91.3 0.7 collective-permute-start.27
  92.0 1.1 %place_got_1.1 = (f32[8,128]{1,0:T(8,128)S(1)}, f32[512,2048]{1,0:T(8,128)}, f32[2048,512]{1,0:T(8,128)}) custom-call(bf16[512,512]{1,0:T(8,128)(2,1)S(1)} %feed_got_1.1.refs_0_.refs_3_, f32[512,2048]{1,0:T(8,128)} %get-tuple-element.204.refs_1_, f32[2048,512]{1,0:T(8,128)} %get-tuple-element.205.refs_2_, ...), custom_call_target="tpu_custom_call", output_to_operand_aliasing={{1}: (1, {}), {2}: (2, {})} | custom-call | flops 10000000000 | bytes 1 | tf_op jit(solution)/shard_map/place_got_1/pallas_call | solution.py:99
  93.5 1.5 %place_far.1 = (f32[8,128]{1,0:T(8,128)S(1)}, f32[512,2048]{1,0:T(8,128)}, f32[2048,512]{1,0:T(8,128)}) custom-call(bf16[512,512]{1,0:T(8,128)(2,1)S(1)} %collective-permute-done.25.refs_0_, bf16[512,512]{1,0:T(8,128)(2,1)S(1)} %collective-permute-done.27.refs_1_, ...), custom_call_target="tpu_custom_call", output_to_operand_aliasing={{1}: (2, {}), {2}: (3, {})} | custom-call | flops 10000000000 | bytes 1 | tf_op jit(solution)/shard_map/place_far/pallas_call | solution.py:99
  95.0 2.5 %collective-permute-done.24.refs_1_ = bf16[352,512]{1,0:T(8,128)(2,1)S(1)} collective-permute-done((bf16[352,512]{1,0:T(8,128)(2,1)S(1)}, bf16[352,512]{1,0:T(8,128)(2,1)S(1)}, u32[]{:S(2)}, u32[]{:S(2)}) %collective-permute-start.24) | collective-permute-done | bytes 360480 | tf_op jit(solution)/shard_map/ppermute | solution.py:889
  97.5 1.2 %finish.1 = (f32[8,128]{1,0:T(8,128)}, f32[256,512]{1,0:T(8,128)}, f32[256,512]{1,0:T(8,128)}, f32[64,512]{1,0:T(8,128)}, f32[64,512]{1,0:T(8,128)}, /*index=5*/...) custom-call(bf16[352,512]{1,0:T(8,128)(2,1)S(1)} %rest_join_1.1.refs, ...), custom_call_target="tpu_custom_call" | custom-call | flops 10000000000 | bytes 1 | tf_op jit(solution)/shard_map/finish/pallas_call | solution.py:99
  (50 shorter events, 5.3 us)
Async XLA Ops:
  0.6 3.6 %collective-permute-start = (bf16[256,512]{1,0:T(8,128)(2,1)}, bf16[256,512]{1,0:T(8,128)(2,1)S(1)}, u32[]{:S(2)}, u32[]{:S(2)}) collective-permute-start(bf16[256,512]{1,0:T(8,128)(2,1)} %bitcast.18), channel_id=1, source_target_pairs={{0,1},{1,0},{2,3},{3,2},{4,5},{5,4},{6,7},{7,6},{8,9},{9,8},{10,11... | collective-permute-start | bytes 786440 | tf_op jit(solution)/shard_map/ppermute | solution.py:552
  1.2 3.1 %collective-permute-start.1 = (bf16[256,512]{1,0:T(8,128)(2,1)}, bf16[256,512]{1,0:T(8,128)(2,1)S(1)}, u32[]{:S(2)}, u32[]{:S(2)}) collective-permute-start(bf16[256,512]{1,0:T(8,128)(2,1)} %bitcast.20), channel_id=1, source_target_pairs={{0,1},{1,0},{2,3},{3,2},{4,5},{5,4},{6,7},{7,6},{8,9},{9,8},{10,11... | collective-permute-start | bytes 786440 | tf_op jit(solution)/shard_map/ppermute | solution.py:552
  4.2 5.5 %copy-start = (bf16[1024,512]{1,0:T(8,128)(2,1)}, bf16[1024,512]{1,0:T(8,128)(2,1)S(1)}, u32[]{:S(2)}) copy-start(bf16[1024,512]{1,0:T(8,128)(2,1)S(1)} %get-tuple-element.120.refs_1_.refs_6_) | copy-start | bytes 3145732
  11.2 2.0 %collective-permute-start.2 = (bf16[512,512]{1,0:T(8,128)(2,1)S(1)}, bf16[512,512]{1,0:T(8,128)(2,1)S(1)}, u32[]{:S(2)}, u32[]{:S(2)}) collective-permute-start(bf16[512,512]{1,0:T(8,128)(2,1)S(1)} %get-tuple-element.139), channel_id=1, source_target_pairs={{0,1},{1,0},{2,3},{3,2},{4,5},{5,4},{6,7},{7,6},{8,9},{9,8},{10,11... | collective-permute-start | bytes 1572872 | tf_op jit(solution)/shard_map/ppermute | solution.py:552
  13.4 17.3 %collective-permute-start.4 = (bf16[512,512]{1,0:T(8,128)(2,1)S(1)}, bf16[512,512]{1,0:T(8,128)(2,1)S(1)}, u32[]{:S(2)}, u32[]{:S(2)}) collective-permute-start(bf16[512,512]{1,0:T(8,128)(2,1)S(1)} %feed_add_0.1.refs_7_), channel_id=1, source_target_pairs={{0,2},{1,5},{2,0},{3,7},{4,6},{5,1},{6,4},{7,3},{8,10},{9,13},{10,... | collective-permute-start | bytes 1572872 | tf_op jit(solution)/shard_map/ppermute | solution.py:798
  17.8 2.0 %collective-permute-start.3 = (bf16[512,512]{1,0:T(8,128)(2,1)S(1)}, bf16[512,512]{1,0:T(8,128)(2,1)S(1)}, u32[]{:S(2)}, u32[]{:S(2)}) collective-permute-start(bf16[512,512]{1,0:T(8,128)(2,1)S(1)} %get-tuple-element.144), channel_id=1, source_target_pairs={{0,1},{1,0},{2,3},{3,2},{4,5},{5,4},{6,7},{7,6},{8,9},{9,8},{10,11... | collective-permute-start | bytes 1572872 | tf_op jit(solution)/shard_map/ppermute | solution.py:552
  19.9 10.8 %collective-permute-start.5 = (bf16[512,512]{1,0:T(8,128)(2,1)S(1)}, bf16[512,512]{1,0:T(8,128)(2,1)S(1)}, u32[]{:S(2)}, u32[]{:S(2)}) collective-permute-start(bf16[512,512]{1,0:T(8,128)(2,1)S(1)} %feed_add_1.1.refs_7_), channel_id=1, source_target_pairs={{0,2},{1,5},{2,0},{3,7},{4,6},{5,1},{6,4},{7,3},{8,10},{9,13},{10,... | collective-permute-start | bytes 1572872 | tf_op jit(solution)/shard_map/ppermute | solution.py:802
  23.7 6.9 %collective-permute-start.6 = (bf16[1024,512]{1,0:T(8,128)(2,1)S(1)}, bf16[1024,512]{1,0:T(8,128)(2,1)S(1)}, u32[]{:S(2)}, u32[]{:S(2)}) collective-permute-start(bf16[1024,512]{1,0:T(8,128)(2,1)S(1)} %get-tuple-element.165), channel_id=1, source_target_pairs={{0,1},{1,0},{2,3},{3,2},{4,5},{5,4},{6,7},{7,6},{8,9},{9,8},{10,11... | collective-permute-start | bytes 3145736 | tf_op jit(solution)/shard_map/ppermute | solution.py:552
  30.9 9.2 %collective-permute-start.8 = (bf16[512,512]{1,0:T(8,128)(2,1)S(1)}, bf16[512,512]{1,0:T(8,128)(2,1)S(1)}, u32[]{:S(2)}, u32[]{:S(2)}) collective-permute-start(bf16[512,512]{1,0:T(8,128)(2,1)S(1)} %feed_send_1.1.refs_11_), channel_id=1, source_target_pairs={{0,4},{1,3},{2,6},{3,1},{4,0},{5,7},{6,2},{7,5},{8,12},{9,11},{10,... | collective-permute-start | bytes 1572872 | tf_op jit(solution)/shard_map/ppermute | solution.py:826
  38.6 6.5 %collective-permute-start.7 = (bf16[704,512]{1,0:T(8,128)(2,1)S(1)}, bf16[704,512]{1,0:T(8,128)(2,1)S(1)}, u32[]{:S(2)}, u32[]{:S(2)}) collective-permute-start(bf16[704,512]{1,0:T(8,128)(2,1)S(1)} %get-tuple-element.185), channel_id=1, source_target_pairs={{0,1},{1,0},{2,3},{3,2},{4,5},{5,4},{6,7},{7,6},{8,9},{9,8},{10,11... | collective-permute-start | bytes 2162696 | tf_op jit(solution)/shard_map/ppermute | solution.py:552
  40.7 12.9 %collective-permute-start.11 = (bf16[512,128]{1,0:T(8,128)(2,1)S(1)}, bf16[512,128]{1,0:T(8,128)(2,1)S(1)}, u32[]{:S(2)}, u32[]{:S(2)}) collective-permute-start(bf16[512,128]{1,0:T(8,128)(2,1)S(1)} %get-tuple-element.189), channel_id=1, source_target_pairs={{0,8},{1,9},{2,10},{3,11},{4,12},{5,13},{6,14},{7,15},{8,0},{9,1},... | collective-permute-start | bytes 393224 | tf_op jit(solution)/shard_map/ppermute | solution.py:871
  42.3 12.4 %collective-permute-start.12 = (bf16[512,128]{1,0:T(8,128)(2,1)S(1)}, bf16[512,128]{1,0:T(8,128)(2,1)S(1)}, u32[]{:S(2)}, u32[]{:S(2)}) collective-permute-start(bf16[512,128]{1,0:T(8,128)(2,1)S(1)} %get-tuple-element.190), channel_id=1, source_target_pairs={{0,16},{1,17},{2,18},{3,19},{4,20},{5,21},{6,22},{7,23},{8,24},{9,... | collective-permute-start | bytes 393224 | tf_op jit(solution)/shard_map/ppermute | solution.py:871
  44.9 9.8 %collective-permute-start.13 = (bf16[512,128]{1,0:T(8,128)(2,1)S(1)}, bf16[512,128]{1,0:T(8,128)(2,1)S(1)}, u32[]{:S(2)}, u32[]{:S(2)}) collective-permute-start(bf16[512,128]{1,0:T(8,128)(2,1)S(1)} %get-tuple-element.191), channel_id=1, source_target_pairs={{0,24},{1,25},{2,26},{3,27},{4,28},{5,29},{6,30},{7,31},{8,16},{9,... | collective-permute-start | bytes 393224 | tf_op jit(solution)/shard_map/ppermute | solution.py:871
  45.2 7.5 %collective-permute-start.9 = (bf16[352,512]{1,0:T(8,128)(2,1)S(1)}, bf16[352,512]{1,0:T(8,128)(2,1)S(1)}, u32[]{:S(2)}, u32[]{:S(2)}) collective-permute-start(bf16[352,512]{1,0:T(8,128)(2,1)S(1)} %rest_send_0.1.refs_12_), channel_id=1, source_target_pairs={{0,2},{1,5},{2,0},{3,7},{4,6},{5,1},{6,4},{7,3},{8,10},{9,13},{10,... | collective-permute-start | bytes 1081352 | tf_op jit(solution)/shard_map/ppermute | solution.py:883
  52.8 6.5 %collective-permute-start.10 = (bf16[176,512]{1,0:T(8,128)(2,1)S(1)}, bf16[176,512]{1,0:T(8,128)(2,1)S(1)}, u32[]{:S(2)}, u32[]{:S(2)}) collective-permute-start(bf16[176,512]{1,0:T(8,128)(2,1)S(1)} %rest_send_1.1.refs_4_), channel_id=1, source_target_pairs={{0,4},{1,3},{2,6},{3,1},{4,0},{5,7},{6,2},{7,5},{8,12},{9,11},{10,... | collective-permute-start | bytes 540680 | tf_op jit(solution)/shard_map/ppermute | solution.py:883
  54.8 5.7 %copy-start.1 = (bf16[1024,512]{1,0:T(8,128)(2,1)S(1)}, bf16[1024,512]{1,0:T(8,128)(2,1)}, u32[]{:S(2)}) copy-start(bf16[1024,512]{1,0:T(8,128)(2,1)} %copy-done) | copy-start | bytes 3145732
  54.8 8.8 %collective-permute-start.17 = (bf16[512,128]{1,0:T(8,128)(2,1)S(1)}, bf16[512,128]{1,0:T(8,128)(2,1)S(1)}, u32[]{:S(2)}, u32[]{:S(2)}) collective-permute-start(bf16[512,128]{1,0:T(8,128)(2,1)S(1)} %feed_sum.1.refs_4_.refs_0_), channel_id=1, source_target_pairs={{0,24},{1,25},{2,26},{3,27},{4,28},{5,29},{6,30},{7,31},{8,16},{9,... | collective-permute-start | bytes 393224 | tf_op jit(solution)/shard_map/ppermute | solution.py:871
  57.3 10.1 %collective-permute-start.16 = (bf16[512,128]{1,0:T(8,128)(2,1)S(1)}, bf16[512,128]{1,0:T(8,128)(2,1)S(1)}, u32[]{:S(2)}, u32[]{:S(2)}) collective-permute-start(bf16[512,128]{1,0:T(8,128)(2,1)S(1)} %feed_sum.1.refs_4_.refs_0_), channel_id=1, source_target_pairs={{0,16},{1,17},{2,18},{3,19},{4,20},{5,21},{6,22},{7,23},{8,24},{9,... | collective-permute-start | bytes 393224 | tf_op jit(solution)/shard_map/ppermute | solution.py:871
  58.3 9.2 %collective-permute-start.15 = (bf16[512,128]{1,0:T(8,128)(2,1)S(1)}, bf16[512,128]{1,0:T(8,128)(2,1)S(1)}, u32[]{:S(2)}, u32[]{:S(2)}) collective-permute-start(bf16[512,128]{1,0:T(8,128)(2,1)S(1)} %feed_sum.1.refs_4_.refs_0_), channel_id=1, source_target_pairs={{0,8},{1,9},{2,10},{3,11},{4,12},{5,13},{6,14},{7,15},{8,0},{9,1},... | collective-permute-start | bytes 393224 | tf_op jit(solution)/shard_map/ppermute | solution.py:871
  59.4 10.4 %collective-permute-start.14 = (bf16[176,512]{1,0:T(8,128)(2,1)S(1)}, bf16[176,512]{1,0:T(8,128)(2,1)S(1)}, u32[]{:S(2)}, u32[]{:S(2)}) collective-permute-start(bf16[176,512]{1,0:T(8,128)(2,1)S(1)} %rest_sum.1.refs_9_.refs_0_), channel_id=1, source_target_pairs={{0,8},{1,9},{2,10},{3,11},{4,12},{5,13},{6,14},{7,15},{8,0},{9,1},... | collective-permute-start | bytes 540680 | tf_op jit(solution)/shard_map/ppermute | solution.py:924
  67.5 6.9 %collective-permute-start.19 = (bf16[256,512]{1,0:T(8,128)(2,1)S(1)}, bf16[256,512]{1,0:T(8,128)(2,1)S(1)}, u32[]{:S(2)}, u32[]{:S(2)}) collective-permute-start(bf16[256,512]{1,0:T(8,128)(2,1)S(1)} %feed_row_0.1.refs_4_.refs_0_), channel_id=1, source_target_pairs={{0,4},{1,3},{2,6},{3,1},{4,0},{5,7},{6,2},{7,5},{8,12},{9,11},{10,... | collective-permute-start | bytes 786440 | tf_op jit(solution)/shard_map/ppermute | solution.py:936
  69.1 11.0 %collective-permute-start.20 = (bf16[256,512]{1,0:T(8,128)(2,1)S(1)}, bf16[256,512]{1,0:T(8,128)(2,1)S(1)}, u32[]{:S(2)}, u32[]{:S(2)}) collective-permute-start(bf16[256,512]{1,0:T(8,128)(2,1)S(1)} %feed_row_1.1.refs_2_.refs_0_), channel_id=1, source_target_pairs={{0,4},{1,3},{2,6},{3,1},{4,0},{5,7},{6,2},{7,5},{8,12},{9,11},{10,... | collective-permute-start | bytes 786440 | tf_op jit(solution)/shard_map/ppermute | solution.py:936
  69.8 13.3 %collective-permute-start.18 = (bf16[176,512]{1,0:T(8,128)(2,1)S(1)}, bf16[176,512]{1,0:T(8,128)(2,1)S(1)}, u32[]{:S(2)}, u32[]{:S(2)}) collective-permute-start(bf16[176,512]{1,0:T(8,128)(2,1)S(1)} %rest_add_0.1.refs_2_.refs_0_), channel_id=1, source_target_pairs={{0,16},{1,17},{2,18},{3,19},{4,20},{5,21},{6,22},{7,23},{8,24},{9,... | collective-permute-start | bytes 540680 | tf_op jit(solution)/shard_map/ppermute | solution.py:938
  74.5 12.8 %collective-permute-start.22 = (bf16[512,512]{1,0:T(8,128)(2,1)S(1)}, bf16[512,512]{1,0:T(8,128)(2,1)S(1)}, u32[]{:S(2)}, u32[]{:S(2)}) collective-permute-start(bf16[512,512]{1,0:T(8,128)(2,1)S(1)} %feed_join_1_0.1.refs_0_.refs_1_), channel_id=1, source_target_pairs={{0,2},{1,5},{2,0},{3,7},{4,6},{5,1},{6,4},{7,3},{8,10},{9,13},{10,... | collective-permute-start | bytes 1572872 | tf_op jit(solution)/shard_map/ppermute | solution.py:889
  80.1 11.2 %collective-permute-start.26 = (bf16[512,512]{1,0:T(8,128)(2,1)S(1)}, bf16[512,512]{1,0:T(8,128)(2,1)S(1)}, u32[]{:S(2)}, u32[]{:S(2)}) collective-permute-start(bf16[512,512]{1,0:T(8,128)(2,1)S(1)} %feed_join_1_1.1.refs_0_.refs_3_.refs_1_), channel_id=1, source_target_pairs={{0,2},{1,5},{2,0},{3,7},{4,6},{5,1},{6,4},{7,3},{8,10},{9,13},{10,... | collective-permute-start | bytes 1572872 | tf_op jit(solution)/shard_map/ppermute | solution.py:889
  83.0 2.7 %collective-permute-start.23 = (bf16[1024,512]{1,0:T(8,128)(2,1)S(1)}, bf16[1024,512]{1,0:T(8,128)(2,1)S(1)}, u32[]{:S(2)}, u32[]{:S(2)}) collective-permute-start(bf16[1024,512]{1,0:T(8,128)(2,1)S(1)} %feed_own.1.refs_2_), channel_id=1, source_target_pairs={{0,1},{1,0},{2,3},{3,2},{4,5},{5,4},{6,7},{7,6},{8,9},{9,8},{10,11... | collective-permute-start | bytes 3145736 | tf_op jit(solution)/shard_map/ppermute | solution.py:552
  83.2 6.8 %collective-permute-start.21 = (bf16[176,512]{1,0:T(8,128)(2,1)S(1)}, bf16[176,512]{1,0:T(8,128)(2,1)S(1)}, u32[]{:S(2)}, u32[]{:S(2)}) collective-permute-start(bf16[176,512]{1,0:T(8,128)(2,1)S(1)} %rest_add_1.1.refs_3_.refs_0_), channel_id=1, source_target_pairs={{0,4},{1,3},{2,6},{3,1},{4,0},{5,7},{6,2},{7,5},{8,12},{9,11},{10,... | collective-permute-start | bytes 540680 | tf_op jit(solution)/shard_map/ppermute | solution.py:948
  87.3 6.2 %collective-permute-start.25 = (bf16[512,512]{1,0:T(8,128)(2,1)S(1)}, bf16[512,512]{1,0:T(8,128)(2,1)S(1)}, u32[]{:S(2)}, u32[]{:S(2)}) collective-permute-start(bf16[512,512]{1,0:T(8,128)(2,1)S(1)} %feed_got_0.1.refs_0_.refs_3_), channel_id=1, source_target_pairs={{0,1},{1,0},{2,3},{3,2},{4,5},{5,4},{6,7},{7,6},{8,9},{9,8},{10,11... | collective-permute-start | bytes 1572872 | tf_op jit(solution)/shard_map/ppermute | solution.py:552
  90.0 7.5 %collective-permute-start.24 = (bf16[352,512]{1,0:T(8,128)(2,1)S(1)}, bf16[352,512]{1,0:T(8,128)(2,1)S(1)}, u32[]{:S(2)}, u32[]{:S(2)}) collective-permute-start(bf16[352,512]{1,0:T(8,128)(2,1)S(1)} %rest_join_1.1.refs_1_.refs_0_), channel_id=1, source_target_pairs={{0,2},{1,5},{2,0},{3,7},{4,6},{5,1},{6,4},{7,3},{8,10},{9,13},{10,... | collective-permute-start | bytes 1081352 | tf_op jit(solution)/shard_map/ppermute | solution.py:889
  91.3 2.2 %collective-permute-start.27 = (bf16[512,512]{1,0:T(8,128)(2,1)S(1)}, bf16[512,512]{1,0:T(8,128)(2,1)S(1)}, u32[]{:S(2)}, u32[]{:S(2)}) collective-permute-start(bf16[512,512]{1,0:T(8,128)(2,1)S(1)} %feed_got_1.1.refs_0_.refs_3_), channel_id=1, source_target_pairs={{0,1},{1,0},{2,3},{3,2},{4,5},{5,4},{6,7},{7,6},{8,9},{9,8},{10,11... | collective-permute-start | bytes 1572872 | tf_op jit(solution)/shard_map/ppermute | solution.py:552
where the time goes:
time: 99 us; the launch traced here: 98.9 us
  Pallas kernels  47.8 us (48%)
  starting transfers between devices  29.2 us (29%)
  waiting for transfers between devices  20.6 us (21%)
  between operations  1.17 us (1%)
    pallas_call x38, Pallas kernels, call(): pl.pallas_call(run, in_specs=[INSIDE] * len(operands) + [ANYWHERE] * (len...  47.8 us
    ppermute x6, starting transfers between devices, across(): lax.ppermute(v, AXES, quad_pairs(n_dp, t + 1))  8.9 us
    ppermute x2, waiting for transfers between devices, local(): got[part] = lax.ppermute(joined[part], AXES, pairs_of(n_dp, steps - 1))  5.77 us
    ppermute x6, waiting for transfers between devices, across(): lax.ppermute(v, AXES, quad_pairs(n_dp, t + 1))  5.02 us
    ppermute x3, starting transfers between devices, join(): return (joined, lax.ppermute(joined, AXES, pairs_of(n_dp, step - 1)))  4.73 us
    ppermute x1, starting transfers between devices, local(): lax.ppermute(add('feed_add_0', mine, swapped), AXES, pairs_of(n_dp, 0))  2.93 us
    ppermute x2, waiting for transfers between devices, rest_send(): rest_terms.append([lax.ppermute(part, AXES, pairs_of(n_dp, step))])  2.79 us
    ppermute x9, starting transfers between devices, core_swap(): return lax.ppermute(values, AXES, [(at, at ^ 1) for at in range(2 * n_dp)])  2.78 us
  transfers between devices with their start and end apart: 28, of which 13 were waited for; matrix products, arithmetic and copies ran while one was open for 0% of the time, Pallas kernels for 40%

commit v1 on v0

--- a/solution.py
+++ b/solution.py
@@ -104,7 +104,7 @@
             scratch_shapes=list(scratch),
             input_output_aliases={len(operands) + a: near + b for a, b in aliases},
             compiler_params=pltpu.CompilerParams(vmem_limit_bytes=VMEM_LIMIT),
-            cost_estimate=pl.CostEstimate(flops=3 * 10**10 if name == "rest_add_1" else 10**10, bytes_accessed=1, transcendentals=0),
+            cost_estimate=pl.CostEstimate(flops=3 * 10**10 if name == "place_got_0" else 10**10, bytes_accessed=1, transcendentals=0),
             name=name,
         )(*operands, *far, *self.before)
         self.before = [result[0]]
@@ -942,11 +942,11 @@
             joined[part], got[part] = join(name, step, joined[part], got[part])
             if step == 1:
                 place(f"place_own_{part}", (6 + part,), [joined[part]])
+                if part == 0:
+                    rest = add("rest_add_1", rest, rest_got)
+                    rest_got = lax.ppermute(rest, AXES, pairs_of(n_dp, steps - 1))
     both = call(stack_kernel, "feed_own", joined, there((2 * width, 2 * cols), LOW))
     other = core_swap(both, n_dp)
-    rest = add("rest_add_1", rest, rest_got)
-    rest_got = lax.ppermute(rest, AXES, pairs_of(n_dp, steps - 1))
-    place("place_other", (4, 5), [other])
     far = []
 
     def place_got(part):
@@ -957,6 +957,7 @@
     place_got(0)
     for step in reversed(range(1, steps)):
         rest, rest_got = join(f"rest_join_{step}", step, rest, rest_got)
+    place("place_other", (4, 5), [other])
     place_got(1)
     place("place_far", (0, 1), far)
     vectors = [there((width,), WIDE)] * 5 + [there((ff,), WIDE)]

time: 99 us -> 96.7 us (0.977)
  waiting for transfers between devices: 20.6 us -> 18.5 us
    ppermute x2, waiting for transfers between devices: 5.77 us -> 3.09 us  [local(): got[part] = lax.ppermute(joined[part], AXES, pairs_of(n_dp, steps - 1))]
    ppermute x1, waiting for transfers between devices: 0.01 us -> 2 us  [local(): rest_got = lax.ppermute(rest, AXES, cross_pairs(n_dp, 1))]
    ppermute x1, waiting for transfers between devices: 1.36 us -> 0.01 us  [local(): rest_got = lax.ppermute(rest, AXES, pairs_of(n_dp, steps - 1))]
  transfers between devices with their start and end apart: 28 -> 28, of which waited for: 13 -> 12; matrix products, arithmetic and copies ran while one was open for 0% -> 0% of each run, Pallas kernels for 40% -> 41%
where the time goes in v1:
time: 96.7 us; the launch traced here: 96.5 us
  Pallas kernels  47.8 us (49%)
  starting transfers between devices  28.9 us (30%)
  waiting for transfers between devices  18.5 us (19%)
  between operations  1.19 us (1%)
    pallas_call x38, Pallas kernels, call(): pl.pallas_call(run, in_specs=[INSIDE] * len(operands) + [ANYWHERE] * (len...  47.8 us
    ppermute x6, starting transfers between devices, across(): lax.ppermute(v, AXES, quad_pairs(n_dp, t + 1))  8.9 us
    ppermute x3, starting transfers between devices, join(): return (joined, lax.ppermute(joined, AXES, pairs_of(n_dp, step - 1)))  5.2 us
    ppermute x6, waiting for transfers between devices, across(): lax.ppermute(v, AXES, quad_pairs(n_dp, t + 1))  5.02 us
    ppermute x2, waiting for transfers between devices, local(): got[part] = lax.ppermute(joined[part], AXES, pairs_of(n_dp, steps - 1))  3.09 us
    ppermute x3, waiting for transfers between devices, join(): return (joined, lax.ppermute(joined, AXES, pairs_of(n_dp, step - 1)))  3.05 us
    ppermute x1, starting transfers between devices, local(): lax.ppermute(add('feed_add_0', mine, swapped), AXES, pairs_of(n_dp, 0))  2.93 us
    ppermute x2, waiting for transfers between devices, rest_send(): rest_terms.append([lax.ppermute(part, AXES, pairs_of(n_dp, step))])  2.79 us
  transfers between devices with their start and end apart: 28, of which 12 were waited for; matrix products, arithmetic and copies ran while one was open for 0% of the time, Pallas kernels for 41%

profile of v1, /device:TPU:0, one launch (start us, length us, event | category | flops | bytes accessed | tf_op | source)
XLA Modules:
  0.0 96.5 jit_solution(15314958745382312721)
XLA Ops:
  1.2 3.0 %first_norm.1 = (bf16[1024,512]{1,0:T(8,128)(2,1)S(1)}, f32[16,512]{1,0:T(8,128)S(1)}, bf16[1024,128]{1,0:T(8,128)(2,1)S(1)}, bf16[64,1024]{1,0:T(8,128)(2,1)S(1...) custom-call(bf16[1024,512]{1,0:T(8,128)(2,1)} %refs_0_.1, ...), custom_call_target="tpu_custom_call" | custom-call | flops 10000000000 | bytes 1 | tf_op jit(solution)/shard_map/first_norm/pallas_call | solution.py:99
  4.2 5.5 %attention_forward.1 = (bf16[1024,2048]{1,0:T(8,128)(2,1)S(1)}, bf16[64,2048]{1,0:T(8,128)(2,1)S(1)}, f32[64,2048]{1,0:T(8,128)S(1)}, f32[8,2048]{1,0:T(8,128)S(...) custom-call(bf16[1024,512]{1,0:T(8,128)(2,1)S(1)} %get-tuple-element, ...), custom_call_target="tpu_custom_call" | custom-call | flops 10000000000 | bytes 1 | tf_op jit(solution)/shard_map/attention_forward/pallas_call | solution.py:99
  9.7 1.5 %feed_0.1 = (bf16[1024,256]{1,0:T(8,128)(2,1)S(1)}, bf16[1024,256]{1,0:T(8,128)(2,1)S(1)}, f32[1,256]{1,0:T(1,128)S(1)}, bf16[512,512]{1,0:T(8,128)(2,1)S(1)}) custom-call(bf16[1024,512]{1,0:T(8,128)(2,1)S(1)} %get-tuple-element.130.refs_0_, bf16[512,1024]{1,0:T(8,128)(2,1)S(1)} %get-tuple-element.131.refs_1_, ...), custom_call_target="tpu_custom_call" | custom-call | flops 10000000000 | bytes 1 | tf_op jit(solution)/shard_map/feed_0/pallas_call | solution.py:99
  11.7 1.5 %feed_2.1 = (bf16[1024,256]{1,0:T(8,128)(2,1)S(1)}, bf16[1024,256]{1,0:T(8,128)(2,1)S(1)}, f32[1,256]{1,0:T(1,128)S(1)}, bf16[512,512]{1,0:T(8,128)(2,1)S(1)}) custom-call(bf16[1024,512]{1,0:T(8,128)(2,1)S(1)} %get-tuple-element.130.refs_0_, bf16[512,1024]{1,0:T(8,128)(2,1)S(1)} %get-tuple-element.131.refs_1_, ...), custom_call_target="tpu_custom_call" | custom-call | flops 10000000000 | bytes 1 | tf_op jit(solution)/shard_map/feed_2/pallas_call | solution.py:99
  13.4 2.9 %collective-permute-start.4 = (bf16[512,512]{1,0:T(8,128)(2,1)S(1)}, bf16[512,512]{1,0:T(8,128)(2,1)S(1)}, u32[]{:S(2)}, u32[]{:S(2)}) collective-permute-start(bf16[512,512]{1,0:T(8,128)(2,1)S(1)} %feed_add_0.1.refs_7_), channel_id=1, source_target_pairs={{0,2},{1,5},{2,0},{3,7},{4,6},{5,1},{6,4},{7,3},{8,10},{9,13},{10,... | collective-permute-start | bytes 1572872 | tf_op jit(solution)/shard_map/ppermute | solution.py:798
  16.3 1.5 %feed_1.1 = (bf16[1024,256]{1,0:T(8,128)(2,1)S(1)}, bf16[1024,256]{1,0:T(8,128)(2,1)S(1)}, f32[1,256]{1,0:T(1,128)S(1)}, bf16[512,512]{1,0:T(8,128)(2,1)S(1)}) custom-call(bf16[1024,512]{1,0:T(8,128)(2,1)S(1)} %get-tuple-element.130.refs_0_, bf16[512,1024]{1,0:T(8,128)(2,1)S(1)} %get-tuple-element.131.refs_1_, ...), custom_call_target="tpu_custom_call" | custom-call | flops 10000000000 | bytes 1 | tf_op jit(solution)/shard_map/feed_1/pallas_call | solution.py:99
  17.9 1.5 %feed_3.1 = (bf16[1024,256]{1,0:T(8,128)(2,1)S(1)}, bf16[1024,256]{1,0:T(8,128)(2,1)S(1)}, f32[1,256]{1,0:T(1,128)S(1)}, bf16[512,512]{1,0:T(8,128)(2,1)S(1)}) custom-call(bf16[1024,512]{1,0:T(8,128)(2,1)S(1)} %get-tuple-element.130.refs_0_, bf16[512,1024]{1,0:T(8,128)(2,1)S(1)} %get-tuple-element.131.refs_1_, ...), custom_call_target="tpu_custom_call" | custom-call | flops 10000000000 | bytes 1 | tf_op jit(solution)/shard_map/feed_3/pallas_call | solution.py:99
  19.9 1.1 %collective-permute-start.5 = (bf16[512,512]{1,0:T(8,128)(2,1)S(1)}, bf16[512,512]{1,0:T(8,128)(2,1)S(1)}, u32[]{:S(2)}, u32[]{:S(2)}) collective-permute-start(bf16[512,512]{1,0:T(8,128)(2,1)S(1)} %feed_add_1.1.refs_7_), channel_id=1, source_target_pairs={{0,2},{1,5},{2,0},{3,7},{4,6},{5,1},{6,4},{7,3},{8,10},{9,13},{10,... | collective-permute-start | bytes 1572872 | tf_op jit(solution)/shard_map/ppermute | solution.py:802
  21.0 2.8 %feed_4.1 = (bf16[1024,256]{1,0:T(8,128)(2,1)S(1)}, bf16[1024,256]{1,0:T(8,128)(2,1)S(1)}, f32[1,256]{1,0:T(1,128)S(1)}, bf16[1024,256]{1,0:T(8,128)(2,1)S(1)}, ...) custom-call(bf16[1024,512]{1,0:T(8,128)(2,1)S(1)} %get-tuple-element.130.refs_0_, ...), custom_call_target="tpu_custom_call" | custom-call | flops 10000000000 | bytes 1 | tf_op jit(solution)/shard_map/feed_4/pallas_call | solution.py:99
  24.2 3.0 %feed_6.1 = (bf16[1024,256]{1,0:T(8,128)(2,1)S(1)}, bf16[1024,256]{1,0:T(8,128)(2,1)S(1)}, f32[1,256]{1,0:T(1,128)S(1)}, bf16[1024,256]{1,0:T(8,128)(2,1)S(1)}, ...) custom-call(bf16[1024,512]{1,0:T(8,128)(2,1)S(1)} %get-tuple-element.130.refs_0_, ...), custom_call_target="tpu_custom_call" | custom-call | flops 10000000000 | bytes 1 | tf_op jit(solution)/shard_map/feed_6/pallas_call | solution.py:99
  27.2 3.5 %second_norm_back.1 = (f32[1024,512]{1,0:T(8,128)S(1)}, bf16[1024,512]{1,0:T(8,128)(2,1)S(1)}, f32[1,512]{1,0:T(1,128)S(1)}, f32[1,512]{1,0:T(1,128)S(1)}) custom-call(bf16[1024,256]{1,0:T(8,128)(2,1)S(1)} %get-tuple-element.150.refs_0_, bf16[1024,256]{1,0:T(8,128)(2,1)S(1)} %get-tuple-element.151.refs_1_, bf16[1024,256]{1,0:T(8,128)(2,1)S(1)} %get-tuple-element.152.refs_2_, ...), custom_call_target="tpu_custom_call" | custom-call | flops 10000000000 | bytes 1 | tf_op jit(solution)/shard_map/second_norm_back/pallas_call | solution.py:99
  30.9 0.8 collective-permute-start.8
  31.7 5.7 %attention_backward.1 = (bf16[656,1024]{1,0:T(8,128)(2,1)S(1)}, f32[512,512]{1,0:T(8,128)S(1)}) custom-call(bf16[1024,512]{1,0:T(8,128)(2,1)S(1)} %get-tuple-element.159.refs_0_, bf16[1024,2048]{1,0:T(8,128)(2,1)S(1)} %get-tuple-element.136.refs_7_.refs_1_, bf16[64,2048]{1,0:T(8,128)(2,1)S(1)} %get-tuple-element.160.refs_2_, ...), custom_call_target="tpu_custom_call" | custom-call | flops 10000000000 | bytes 1 | tf_op jit(solution)/shard_map/attention_backward/pallas_call | solution.py:99
  37.4 1.2 %projection_grads.1 = (bf16[704,512]{1,0:T(8,128)(2,1)S(1)}, bf16[704,512]{1,0:T(8,128)(2,1)S(1)}) custom-call(bf16[656,1024]{1,0:T(8,128)(2,1)S(1)} %get-tuple-element.168.refs_0_.refs_20_, f32[512,512]{1,0:T(8,128)S(1)} %get-tuple-element.169.refs_1_, bf16[256,512]{1,0:T(8,128)(2,1)S(1)} %get-tuple-element.122.refs_3_.refs_2_.refs_1_, ...), custom_call_target="tpu_custom_call" | custom-call | flops 10000000000 | bytes 1 | tf_op jit(solution)/shard_map/projection_grads/pallas_call | solution.py:99
  38.9 1.3 %collective-permute-done.8.refs_4_ = bf16[512,512]{1,0:T(8,128)(2,1)S(1)} collective-permute-done((bf16[512,512]{1,0:T(8,128)(2,1)S(1)}, bf16[512,512]{1,0:T(8,128)(2,1)S(1)}, u32[]{:S(2)}, u32[]{:S(2)}) %collective-permute-start.8) | collective-permute-done | bytes 524320 | tf_op jit(solution)/shard_map/ppermute | solution.py:826
  40.1 0.5 feed_cut.1
  40.7 1.6 %collective-permute-start.11 = (bf16[512,128]{1,0:T(8,128)(2,1)S(1)}, bf16[512,128]{1,0:T(8,128)(2,1)S(1)}, u32[]{:S(2)}, u32[]{:S(2)}) collective-permute-start(bf16[512,128]{1,0:T(8,128)(2,1)S(1)} %get-tuple-element.189), channel_id=1, source_target_pairs={{0,8},{1,9},{2,10},{3,11},{4,12},{5,13},{6,14},{7,15},{8,0},{9,1},... | collective-permute-start | bytes 393224 | tf_op jit(solution)/shard_map/ppermute | solution.py:871
  42.3 2.6 %collective-permute-start.12 = (bf16[512,128]{1,0:T(8,128)(2,1)S(1)}, bf16[512,128]{1,0:T(8,128)(2,1)S(1)}, u32[]{:S(2)}, u32[]{:S(2)}) collective-permute-start(bf16[512,128]{1,0:T(8,128)(2,1)S(1)} %get-tuple-element.190), channel_id=1, source_target_pairs={{0,16},{1,17},{2,18},{3,19},{4,20},{5,21},{6,22},{7,23},{8,24},{9,... | collective-permute-start | bytes 393224 | tf_op jit(solution)/shard_map/ppermute | solution.py:871
  45.2 0.7 collective-permute-start.9
  45.9 4.0 %layer_out.1 = (f32[8,128]{1,0:T(8,128)S(1)}, f32[1024,512]{1,0:T(8,128)}) custom-call(bf16[1024,256]{1,0:T(8,128)(2,1)S(1)} %get-tuple-element.137.refs_7_.refs_0_, bf16[1024,256]{1,0:T(8,128)(2,1)S(1)} %get-tuple-element.141.refs_7_.refs_1_, bf16[1024,256]{1,0:T(8,128)(2,1)S(1)} %get-tuple-element.140.refs_2_, ...), custom_call_target="tpu_custom_call" | custom-call | flops 10000000000 | bytes 1 | tf_op jit(solution)/shard_map/layer_out/pallas_call | solution.py:99
  49.9 2.8 %collective-permute-done.9.refs_2_ = bf16[352,512]{1,0:T(8,128)(2,1)S(1)} collective-permute-done((bf16[352,512]{1,0:T(8,128)(2,1)S(1)}, bf16[352,512]{1,0:T(8,128)(2,1)S(1)}, u32[]{:S(2)}, u32[]{:S(2)}) %collective-permute-start.9) | collective-permute-done | bytes 360480 | tf_op jit(solution)/shard_map/ppermute | solution.py:883
  52.8 0.8 collective-permute-start.10
  53.6 1.1 %collective-permute-done.12.refs_2_ = bf16[512,128]{1,0:T(8,128)(2,1)S(1)} collective-permute-done((bf16[512,128]{1,0:T(8,128)(2,1)S(1)}, bf16[512,128]{1,0:T(8,128)(2,1)S(1)}, u32[]{:S(2)}, u32[]{:S(2)}) %collective-permute-start.12) | collective-permute-done | bytes 131104 | tf_op jit(solution)/shard_map/ppermute | solution.py:871
  54.8 2.5 %collective-permute-start.17 = (bf16[512,128]{1,0:T(8,128)(2,1)S(1)}, bf16[512,128]{1,0:T(8,128)(2,1)S(1)}, u32[]{:S(2)}, u32[]{:S(2)}) collective-permute-start(bf16[512,128]{1,0:T(8,128)(2,1)S(1)} %feed_sum.1.refs_4_.refs_0_), channel_id=1, source_target_pairs={{0,24},{1,25},{2,26},{3,27},{4,28},{5,29},{6,30},{7,31},{8,16},{9,... | collective-permute-start | bytes 393224 | tf_op jit(solution)/shard_map/ppermute | solution.py:871
  57.3 1.0 collective-permute-start.16
  58.3 1.0 collective-permute-start.15
  59.4 1.1 %collective-permute-start.14 = (bf16[176,512]{1,0:T(8,128)(2,1)S(1)}, bf16[176,512]{1,0:T(8,128)(2,1)S(1)}, u32[]{:S(2)}, u32[]{:S(2)}) collective-permute-start(bf16[176,512]{1,0:T(8,128)(2,1)S(1)} %rest_sum.1.refs_9_.refs_0_), channel_id=1, source_target_pairs={{0,8},{1,9},{2,10},{3,11},{4,12},{5,13},{6,14},{7,15},{8,0},{9,1},... | collective-permute-start | bytes 540680 | tf_op jit(solution)/shard_map/ppermute | solution.py:924
  60.5 3.1 %first_norm_back.1 = (f32[8,128]{1,0:T(8,128)S(1)}, f32[1024,512]{1,0:T(8,128)}) custom-call(bf16[656,1024]{1,0:T(8,128)(2,1)S(1)} %get-tuple-element.168.refs_0_.refs_20_, bf16[256,512]{1,0:T(8,128)(2,1)S(1)} %get-tuple-element.122.refs_3_.refs_2_.refs_1_, bf16[256,512]{1,0:T(8,128)(2,1)S(1)} %collective-permute-done.refs_4_.refs_3_.refs_2_, ...), custom_call_target="tpu_custom_call" | custom-call | flops 10000000000 | bytes 1 | tf_op jit(solution)/shard_map/first_norm_back/pallas_call | solution.py:99
  63.6 3.8 %collective-permute-done.16.refs_2_ = bf16[512,128]{1,0:T(8,128)(2,1)S(1)} collective-permute-done((bf16[512,128]{1,0:T(8,128)(2,1)S(1)}, bf16[512,128]{1,0:T(8,128)(2,1)S(1)}, u32[]{:S(2)}, u32[]{:S(2)}) %collective-permute-start.16) | collective-permute-done | bytes 131104 | tf_op jit(solution)/shard_map/ppermute | solution.py:871
  67.5 1.5 %collective-permute-start.19 = (bf16[256,512]{1,0:T(8,128)(2,1)S(1)}, bf16[256,512]{1,0:T(8,128)(2,1)S(1)}, u32[]{:S(2)}, u32[]{:S(2)}) collective-permute-start(bf16[256,512]{1,0:T(8,128)(2,1)S(1)} %feed_row_0.1.refs_4_.refs_0_), channel_id=1, source_target_pairs={{0,4},{1,3},{2,6},{3,1},{4,0},{5,7},{6,2},{7,5},{8,12},{9,11},{10,... | collective-permute-start | bytes 786440 | tf_op jit(solution)/shard_map/ppermute | solution.py:936
  69.1 0.7 collective-permute-start.22
  69.8 1.5 %collective-permute-start.18 = (bf16[176,512]{1,0:T(8,128)(2,1)S(1)}, bf16[176,512]{1,0:T(8,128)(2,1)S(1)}, u32[]{:S(2)}, u32[]{:S(2)}) collective-permute-start(bf16[176,512]{1,0:T(8,128)(2,1)S(1)} %rest_add_0.1.refs_2_.refs_0_), channel_id=1, source_target_pairs={{0,16},{1,17},{2,18},{3,19},{4,20},{5,21},{6,22},{7,23},{8,24},{9,... | collective-permute-start | bytes 540680 | tf_op jit(solution)/shard_map/ppermute | solution.py:938
  71.3 3.1 %collective-permute-done.19.refs_1_ = bf16[256,512]{1,0:T(8,128)(2,1)S(1)} collective-permute-done((bf16[256,512]{1,0:T(8,128)(2,1)S(1)}, bf16[256,512]{1,0:T(8,128)(2,1)S(1)}, u32[]{:S(2)}, u32[]{:S(2)}) %collective-permute-start.19) | collective-permute-done | bytes 262176 | tf_op jit(solution)/shard_map/ppermute | solution.py:936
  74.5 1.8 %collective-permute-start.21 = (bf16[512,512]{1,0:T(8,128)(2,1)S(1)}, bf16[512,512]{1,0:T(8,128)(2,1)S(1)}, u32[]{:S(2)}, u32[]{:S(2)}) collective-permute-start(bf16[512,512]{1,0:T(8,128)(2,1)S(1)} %feed_join_1_0.1.refs_0_.refs_1_), channel_id=1, source_target_pairs={{0,2},{1,5},{2,0},{3,7},{4,6},{5,1},{6,4},{7,3},{8,10},{9,13},{10,... | collective-permute-start | bytes 1572872 | tf_op jit(solution)/shard_map/ppermute | solution.py:889
  76.2 1.1 %place_own_0.1 = (f32[8,128]{1,0:T(8,128)S(1)}, f32[512,2048]{1,0:T(8,128)}, f32[2048,512]{1,0:T(8,128)}) custom-call(bf16[512,512]{1,0:T(8,128)(2,1)S(1)} %feed_join_1_0.1.refs_0_.refs_1_, bf16[512,512]{1,0:T(8,128)(2,1)S(1)} %feed_join_1_0.1.refs_0_.refs_1_), custom_call_target="tpu_custom_call" | custom-call | flops 10000000000 | bytes 1 | tf_op jit(solution)/shard_map/place_own_0/pallas_call | solution.py:99
  77.3 2.0 %collective-permute-done.18.refs_1_ = bf16[176,512]{1,0:T(8,128)(2,1)S(1)} collective-permute-done((bf16[176,512]{1,0:T(8,128)(2,1)S(1)}, bf16[176,512]{1,0:T(8,128)(2,1)S(1)}, u32[]{:S(2)}, u32[]{:S(2)}) %collective-permute-start.18) | collective-permute-done | bytes 180256 | tf_op jit(solution)/shard_map/ppermute | solution.py:938
  79.4 1.7 %collective-permute-start.20 = (bf16[176,512]{1,0:T(8,128)(2,1)S(1)}, bf16[176,512]{1,0:T(8,128)(2,1)S(1)}, u32[]{:S(2)}, u32[]{:S(2)}) collective-permute-start(bf16[176,512]{1,0:T(8,128)(2,1)S(1)} %rest_add_1.1.refs_2_.refs_0_), channel_id=1, source_target_pairs={{0,4},{1,3},{2,6},{3,1},{4,0},{5,7},{6,2},{7,5},{8,12},{9,11},{10,... | collective-permute-start | bytes 540680 | tf_op jit(solution)/shard_map/ppermute | solution.py:947
  81.2 1.5 %collective-permute-start.25 = (bf16[512,512]{1,0:T(8,128)(2,1)S(1)}, bf16[512,512]{1,0:T(8,128)(2,1)S(1)}, u32[]{:S(2)}, u32[]{:S(2)}) collective-permute-start(bf16[512,512]{1,0:T(8,128)(2,1)S(1)} %feed_join_1_1.1.refs_0_.refs_3_.refs_1_), channel_id=1, source_target_pairs={{0,2},{1,5},{2,0},{3,7},{4,6},{5,1},{6,4},{7,3},{8,10},{9,13},{10,... | collective-permute-start | bytes 1572872 | tf_op jit(solution)/shard_map/ppermute | solution.py:889
  82.6 1.1 %place_own_1.1 = (f32[8,128]{1,0:T(8,128)S(1)}, f32[512,2048]{1,0:T(8,128)}, f32[2048,512]{1,0:T(8,128)}) custom-call(bf16[512,512]{1,0:T(8,128)(2,1)S(1)} %feed_join_1_1.1.refs_0_.refs_3_.refs_1_, f32[512,2048]{1,0:T(8,128)} %get-tuple-element.195.refs_1_, f32[2048,512]{1,0:T(8,128)} %get-tuple-element.196.refs_2_, ...), custom_call_target="tpu_custom_call", output_to_operand_aliasing={{1}: (1, {}), {2}: (2, {})} | custom-call | flops 10000000000 | bytes 1 | tf_op jit(solution)/shard_map/place_own_1/pallas_call | solution.py:99
  83.9 1.7 %collective-permute-done.21.refs_0_ = bf16[512,512]{1,0:T(8,128)(2,1)S(1)} collective-permute-done((bf16[512,512]{1,0:T(8,128)(2,1)S(1)}, bf16[512,512]{1,0:T(8,128)(2,1)S(1)}, u32[]{:S(2)}, u32[]{:S(2)}) %collective-permute-start.21) | collective-permute-done | bytes 524320 | tf_op jit(solution)/shard_map/ppermute | solution.py:889
  85.8 1.1 %place_got_0.1 = (f32[8,128]{1,0:T(8,128)S(1)}, f32[512,2048]{1,0:T(8,128)}, f32[2048,512]{1,0:T(8,128)}) custom-call(bf16[512,512]{1,0:T(8,128)(2,1)S(1)} %feed_got_0.1.refs_0_.refs_3_, f32[512,2048]{1,0:T(8,128)} %get-tuple-element.198.refs_1_, f32[2048,512]{1,0:T(8,128)} %get-tuple-element.199.refs_2_, ...), custom_call_target="tpu_custom_call", output_to_operand_aliasing={{1}: (1, {}), {2}: (2, {})} | custom-call | flops 30000001024 | bytes 1 | tf_op jit(solution)/shard_map/place_got_0/pallas_call | solution.py:99
  86.9 1.9 %collective-permute-start.23 = (bf16[352,512]{1,0:T(8,128)(2,1)S(1)}, bf16[352,512]{1,0:T(8,128)(2,1)S(1)}, u32[]{:S(2)}, u32[]{:S(2)}) collective-permute-start(bf16[352,512]{1,0:T(8,128)(2,1)S(1)} %rest_join_1.1.refs_3_.refs_0_), channel_id=1, source_target_pairs={{0,2},{1,5},{2,0},{3,7},{4,6},{5,1},{6,4},{7,3},{8,10},{9,13},{10,... | collective-permute-start | bytes 1081352 | tf_op jit(solution)/shard_map/ppermute | solution.py:889
  88.9 1.5 %place_other.1 = (f32[8,128]{1,0:T(8,128)S(1)}, f32[512,2048]{1,0:T(8,128)}, f32[2048,512]{1,0:T(8,128)}) custom-call(bf16[1024,512]{1,0:T(8,128)(2,1)S(1)} %collective-permute-done.26.refs_0_, f32[512,2048]{1,0:T(8,128)} %get-tuple-element.201.refs_1_, f32[2048,512]{1,0:T(8,128)} %get-tuple-element.202.refs_2_, ...), custom_call_target="tpu_custom_call", output_to_operand_aliasing={{1}: (1, {}), {2}: (2, {})} | custom-call | flops 10000000000 | bytes 1 | tf_op jit(solution)/shard_map/place_other/pallas_call | solution.py:99
  90.3 0.9 collective-permute-done.25.refs_0_
  91.4 1.1 %place_got_1.1 = (f32[8,128]{1,0:T(8,128)S(1)}, f32[512,2048]{1,0:T(8,128)}, f32[2048,512]{1,0:T(8,128)}) custom-call(bf16[512,512]{1,0:T(8,128)(2,1)S(1)} %feed_got_1.1.refs_0_.refs_3_, f32[512,2048]{1,0:T(8,128)} %get-tuple-element.204.refs_1_, f32[2048,512]{1,0:T(8,128)} %get-tuple-element.205.refs_2_, ...), custom_call_target="tpu_custom_call", output_to_operand_aliasing={{1}: (1, {}), {2}: (2, {})} | custom-call | flops 10000000000 | bytes 1 | tf_op jit(solution)/shard_map/place_got_1/pallas_call | solution.py:99
  92.5 0.8 collective-permute-done.27.refs_1_
  93.3 1.5 %place_far.1 = (f32[8,128]{1,0:T(8,128)S(1)}, f32[512,2048]{1,0:T(8,128)}, f32[2048,512]{1,0:T(8,128)}) custom-call(bf16[512,512]{1,0:T(8,128)(2,1)S(1)} %collective-permute-done.24.refs_0_, bf16[512,512]{1,0:T(8,128)(2,1)S(1)} %collective-permute-done.27.refs_1_, ...), custom_call_target="tpu_custom_call", output_to_operand_aliasing={{1}: (2, {}), {2}: (3, {})} | custom-call | flops 10000000000 | bytes 1 | tf_op jit(solution)/shard_map/place_far/pallas_call | solution.py:99
  95.1 1.2 %finish.1 = (f32[8,128]{1,0:T(8,128)}, f32[256,512]{1,0:T(8,128)}, f32[256,512]{1,0:T(8,128)}, f32[64,512]{1,0:T(8,128)}, f32[64,512]{1,0:T(8,128)}, /*index=5*/...) custom-call(bf16[352,512]{1,0:T(8,128)(2,1)S(1)} %rest_join_1.1.refs, ...), custom_call_target="tpu_custom_call" | custom-call | flops 10000000000 | bytes 1 | tf_op jit(solution)/shard_map/finish/pallas_call | solution.py:99
  (50 shorter events, 4.5 us)
Async XLA Ops:
  0.6 3.6 %collective-permute-start = (bf16[256,512]{1,0:T(8,128)(2,1)}, bf16[256,512]{1,0:T(8,128)(2,1)S(1)}, u32[]{:S(2)}, u32[]{:S(2)}) collective-permute-start(bf16[256,512]{1,0:T(8,128)(2,1)} %bitcast.18), channel_id=1, source_target_pairs={{0,1},{1,0},{2,3},{3,2},{4,5},{5,4},{6,7},{7,6},{8,9},{9,8},{10,11... | collective-permute-start | bytes 786440 | tf_op jit(solution)/shard_map/ppermute | solution.py:552
  1.2 3.1 %collective-permute-start.1 = (bf16[256,512]{1,0:T(8,128)(2,1)}, bf16[256,512]{1,0:T(8,128)(2,1)S(1)}, u32[]{:S(2)}, u32[]{:S(2)}) collective-permute-start(bf16[256,512]{1,0:T(8,128)(2,1)} %bitcast.20), channel_id=1, source_target_pairs={{0,1},{1,0},{2,3},{3,2},{4,5},{5,4},{6,7},{7,6},{8,9},{9,8},{10,11... | collective-permute-start | bytes 786440 | tf_op jit(solution)/shard_map/ppermute | solution.py:552
  4.2 5.5 %copy-start = (bf16[1024,512]{1,0:T(8,128)(2,1)}, bf16[1024,512]{1,0:T(8,128)(2,1)S(1)}, u32[]{:S(2)}) copy-start(bf16[1024,512]{1,0:T(8,128)(2,1)S(1)} %get-tuple-element.120.refs_1_.refs_6_) | copy-start | bytes 3145732
  11.2 2.0 %collective-permute-start.2 = (bf16[512,512]{1,0:T(8,128)(2,1)S(1)}, bf16[512,512]{1,0:T(8,128)(2,1)S(1)}, u32[]{:S(2)}, u32[]{:S(2)}) collective-permute-start(bf16[512,512]{1,0:T(8,128)(2,1)S(1)} %get-tuple-element.139), channel_id=1, source_target_pairs={{0,1},{1,0},{2,3},{3,2},{4,5},{5,4},{6,7},{7,6},{8,9},{9,8},{10,11... | collective-permute-start | bytes 1572872 | tf_op jit(solution)/shard_map/ppermute | solution.py:552
  13.4 17.3 %collective-permute-start.4 = (bf16[512,512]{1,0:T(8,128)(2,1)S(1)}, bf16[512,512]{1,0:T(8,128)(2,1)S(1)}, u32[]{:S(2)}, u32[]{:S(2)}) collective-permute-start(bf16[512,512]{1,0:T(8,128)(2,1)S(1)} %feed_add_0.1.refs_7_), channel_id=1, source_target_pairs={{0,2},{1,5},{2,0},{3,7},{4,6},{5,1},{6,4},{7,3},{8,10},{9,13},{10,... | collective-permute-start | bytes 1572872 | tf_op jit(solution)/shard_map/ppermute | solution.py:798
  17.8 2.0 %collective-permute-start.3 = (bf16[512,512]{1,0:T(8,128)(2,1)S(1)}, bf16[512,512]{1,0:T(8,128)(2,1)S(1)}, u32[]{:S(2)}, u32[]{:S(2)}) collective-permute-start(bf16[512,512]{1,0:T(8,128)(2,1)S(1)} %get-tuple-element.144), channel_id=1, source_target_pairs={{0,1},{1,0},{2,3},{3,2},{4,5},{5,4},{6,7},{7,6},{8,9},{9,8},{10,11... | collective-permute-start | bytes 1572872 | tf_op jit(solution)/shard_map/ppermute | solution.py:552
  19.9 10.8 %collective-permute-start.5 = (bf16[512,512]{1,0:T(8,128)(2,1)S(1)}, bf16[512,512]{1,0:T(8,128)(2,1)S(1)}, u32[]{:S(2)}, u32[]{:S(2)}) collective-permute-start(bf16[512,512]{1,0:T(8,128)(2,1)S(1)} %feed_add_1.1.refs_7_), channel_id=1, source_target_pairs={{0,2},{1,5},{2,0},{3,7},{4,6},{5,1},{6,4},{7,3},{8,10},{9,13},{10,... | collective-permute-start | bytes 1572872 | tf_op jit(solution)/shard_map/ppermute | solution.py:802
  23.7 6.9 %collective-permute-start.6 = (bf16[1024,512]{1,0:T(8,128)(2,1)S(1)}, bf16[1024,512]{1,0:T(8,128)(2,1)S(1)}, u32[]{:S(2)}, u32[]{:S(2)}) collective-permute-start(bf16[1024,512]{1,0:T(8,128)(2,1)S(1)} %get-tuple-element.165), channel_id=1, source_target_pairs={{0,1},{1,0},{2,3},{3,2},{4,5},{5,4},{6,7},{7,6},{8,9},{9,8},{10,11... | collective-permute-start | bytes 3145736 | tf_op jit(solution)/shard_map/ppermute | solution.py:552
  30.9 9.2 %collective-permute-start.8 = (bf16[512,512]{1,0:T(8,128)(2,1)S(1)}, bf16[512,512]{1,0:T(8,128)(2,1)S(1)}, u32[]{:S(2)}, u32[]{:S(2)}) collective-permute-start(bf16[512,512]{1,0:T(8,128)(2,1)S(1)} %feed_send_1.1.refs_11_), channel_id=1, source_target_pairs={{0,4},{1,3},{2,6},{3,1},{4,0},{5,7},{6,2},{7,5},{8,12},{9,11},{10,... | collective-permute-start | bytes 1572872 | tf_op jit(solution)/shard_map/ppermute | solution.py:826
  38.6 6.5 %collective-permute-start.7 = (bf16[704,512]{1,0:T(8,128)(2,1)S(1)}, bf16[704,512]{1,0:T(8,128)(2,1)S(1)}, u32[]{:S(2)}, u32[]{:S(2)}) collective-permute-start(bf16[704,512]{1,0:T(8,128)(2,1)S(1)} %get-tuple-element.185), channel_id=1, source_target_pairs={{0,1},{1,0},{2,3},{3,2},{4,5},{5,4},{6,7},{7,6},{8,9},{9,8},{10,11... | collective-permute-start | bytes 2162696 | tf_op jit(solution)/shard_map/ppermute | solution.py:552
  40.7 12.9 %collective-permute-start.11 = (bf16[512,128]{1,0:T(8,128)(2,1)S(1)}, bf16[512,128]{1,0:T(8,128)(2,1)S(1)}, u32[]{:S(2)}, u32[]{:S(2)}) collective-permute-start(bf16[512,128]{1,0:T(8,128)(2,1)S(1)} %get-tuple-element.189), channel_id=1, source_target_pairs={{0,8},{1,9},{2,10},{3,11},{4,12},{5,13},{6,14},{7,15},{8,0},{9,1},... | collective-permute-start | bytes 393224 | tf_op jit(solution)/shard_map/ppermute | solution.py:871
  42.3 12.4 %collective-permute-start.12 = (bf16[512,128]{1,0:T(8,128)(2,1)S(1)}, bf16[512,128]{1,0:T(8,128)(2,1)S(1)}, u32[]{:S(2)}, u32[]{:S(2)}) collective-permute-start(bf16[512,128]{1,0:T(8,128)(2,1)S(1)} %get-tuple-element.190), channel_id=1, source_target_pairs={{0,16},{1,17},{2,18},{3,19},{4,20},{5,21},{6,22},{7,23},{8,24},{9,... | collective-permute-start | bytes 393224 | tf_op jit(solution)/shard_map/ppermute | solution.py:871
  44.9 9.8 %collective-permute-start.13 = (bf16[512,128]{1,0:T(8,128)(2,1)S(1)}, bf16[512,128]{1,0:T(8,128)(2,1)S(1)}, u32[]{:S(2)}, u32[]{:S(2)}) collective-permute-start(bf16[512,128]{1,0:T(8,128)(2,1)S(1)} %get-tuple-element.191), channel_id=1, source_target_pairs={{0,24},{1,25},{2,26},{3,27},{4,28},{5,29},{6,30},{7,31},{8,16},{9,... | collective-permute-start | bytes 393224 | tf_op jit(solution)/shard_map/ppermute | solution.py:871
  45.2 7.5 %collective-permute-start.9 = (bf16[352,512]{1,0:T(8,128)(2,1)S(1)}, bf16[352,512]{1,0:T(8,128)(2,1)S(1)}, u32[]{:S(2)}, u32[]{:S(2)}) collective-permute-start(bf16[352,512]{1,0:T(8,128)(2,1)S(1)} %rest_send_0.1.refs_12_), channel_id=1, source_target_pairs={{0,2},{1,5},{2,0},{3,7},{4,6},{5,1},{6,4},{7,3},{8,10},{9,13},{10,... | collective-permute-start | bytes 1081352 | tf_op jit(solution)/shard_map/ppermute | solution.py:883
  52.8 6.5 %collective-permute-start.10 = (bf16[176,512]{1,0:T(8,128)(2,1)S(1)}, bf16[176,512]{1,0:T(8,128)(2,1)S(1)}, u32[]{:S(2)}, u32[]{:S(2)}) collective-permute-start(bf16[176,512]{1,0:T(8,128)(2,1)S(1)} %rest_send_1.1.refs_4_), channel_id=1, source_target_pairs={{0,4},{1,3},{2,6},{3,1},{4,0},{5,7},{6,2},{7,5},{8,12},{9,11},{10,... | collective-permute-start | bytes 540680 | tf_op jit(solution)/shard_map/ppermute | solution.py:883
  54.8 5.7 %copy-start.1 = (bf16[1024,512]{1,0:T(8,128)(2,1)S(1)}, bf16[1024,512]{1,0:T(8,128)(2,1)}, u32[]{:S(2)}) copy-start(bf16[1024,512]{1,0:T(8,128)(2,1)} %copy-done) | copy-start | bytes 3145732
  54.8 8.8 %collective-permute-start.17 = (bf16[512,128]{1,0:T(8,128)(2,1)S(1)}, bf16[512,128]{1,0:T(8,128)(2,1)S(1)}, u32[]{:S(2)}, u32[]{:S(2)}) collective-permute-start(bf16[512,128]{1,0:T(8,128)(2,1)S(1)} %feed_sum.1.refs_4_.refs_0_), channel_id=1, source_target_pairs={{0,24},{1,25},{2,26},{3,27},{4,28},{5,29},{6,30},{7,31},{8,16},{9,... | collective-permute-start | bytes 393224 | tf_op jit(solution)/shard_map/ppermute | solution.py:871
  57.3 10.1 %collective-permute-start.16 = (bf16[512,128]{1,0:T(8,128)(2,1)S(1)}, bf16[512,128]{1,0:T(8,128)(2,1)S(1)}, u32[]{:S(2)}, u32[]{:S(2)}) collective-permute-start(bf16[512,128]{1,0:T(8,128)(2,1)S(1)} %feed_sum.1.refs_4_.refs_0_), channel_id=1, source_target_pairs={{0,16},{1,17},{2,18},{3,19},{4,20},{5,21},{6,22},{7,23},{8,24},{9,... | collective-permute-start | bytes 393224 | tf_op jit(solution)/shard_map/ppermute | solution.py:871
  58.3 9.2 %collective-permute-start.15 = (bf16[512,128]{1,0:T(8,128)(2,1)S(1)}, bf16[512,128]{1,0:T(8,128)(2,1)S(1)}, u32[]{:S(2)}, u32[]{:S(2)}) collective-permute-start(bf16[512,128]{1,0:T(8,128)(2,1)S(1)} %feed_sum.1.refs_4_.refs_0_), channel_id=1, source_target_pairs={{0,8},{1,9},{2,10},{3,11},{4,12},{5,13},{6,14},{7,15},{8,0},{9,1},... | collective-permute-start | bytes 393224 | tf_op jit(solution)/shard_map/ppermute | solution.py:871
  59.4 10.4 %collective-permute-start.14 = (bf16[176,512]{1,0:T(8,128)(2,1)S(1)}, bf16[176,512]{1,0:T(8,128)(2,1)S(1)}, u32[]{:S(2)}, u32[]{:S(2)}) collective-permute-start(bf16[176,512]{1,0:T(8,128)(2,1)S(1)} %rest_sum.1.refs_9_.refs_0_), channel_id=1, source_target_pairs={{0,8},{1,9},{2,10},{3,11},{4,12},{5,13},{6,14},{7,15},{8,0},{9,1},... | collective-permute-start | bytes 540680 | tf_op jit(solution)/shard_map/ppermute | solution.py:924
  67.5 6.9 %collective-permute-start.19 = (bf16[256,512]{1,0:T(8,128)(2,1)S(1)}, bf16[256,512]{1,0:T(8,128)(2,1)S(1)}, u32[]{:S(2)}, u32[]{:S(2)}) collective-permute-start(bf16[256,512]{1,0:T(8,128)(2,1)S(1)} %feed_row_0.1.refs_4_.refs_0_), channel_id=1, source_target_pairs={{0,4},{1,3},{2,6},{3,1},{4,0},{5,7},{6,2},{7,5},{8,12},{9,11},{10,... | collective-permute-start | bytes 786440 | tf_op jit(solution)/shard_map/ppermute | solution.py:936
  69.1 12.0 %collective-permute-start.22 = (bf16[256,512]{1,0:T(8,128)(2,1)S(1)}, bf16[256,512]{1,0:T(8,128)(2,1)S(1)}, u32[]{:S(2)}, u32[]{:S(2)}) collective-permute-start(bf16[256,512]{1,0:T(8,128)(2,1)S(1)} %feed_row_1.1.refs_2_.refs_0_), channel_id=1, source_target_pairs={{0,4},{1,3},{2,6},{3,1},{4,0},{5,7},{6,2},{7,5},{8,12},{9,11},{10,... | collective-permute-start | bytes 786440 | tf_op jit(solution)/shard_map/ppermute | solution.py:936
  69.8 9.5 %collective-permute-start.18 = (bf16[176,512]{1,0:T(8,128)(2,1)S(1)}, bf16[176,512]{1,0:T(8,128)(2,1)S(1)}, u32[]{:S(2)}, u32[]{:S(2)}) collective-permute-start(bf16[176,512]{1,0:T(8,128)(2,1)S(1)} %rest_add_0.1.refs_2_.refs_0_), channel_id=1, source_target_pairs={{0,16},{1,17},{2,18},{3,19},{4,20},{5,21},{6,22},{7,23},{8,24},{9,... | collective-permute-start | bytes 540680 | tf_op jit(solution)/shard_map/ppermute | solution.py:938
  74.5 11.2 %collective-permute-start.21 = (bf16[512,512]{1,0:T(8,128)(2,1)S(1)}, bf16[512,512]{1,0:T(8,128)(2,1)S(1)}, u32[]{:S(2)}, u32[]{:S(2)}) collective-permute-start(bf16[512,512]{1,0:T(8,128)(2,1)S(1)} %feed_join_1_0.1.refs_0_.refs_1_), channel_id=1, source_target_pairs={{0,2},{1,5},{2,0},{3,7},{4,6},{5,1},{6,4},{7,3},{8,10},{9,13},{10,... | collective-permute-start | bytes 1572872 | tf_op jit(solution)/shard_map/ppermute | solution.py:889
  79.4 7.5 %collective-permute-start.20 = (bf16[176,512]{1,0:T(8,128)(2,1)S(1)}, bf16[176,512]{1,0:T(8,128)(2,1)S(1)}, u32[]{:S(2)}, u32[]{:S(2)}) collective-permute-start(bf16[176,512]{1,0:T(8,128)(2,1)S(1)} %rest_add_1.1.refs_2_.refs_0_), channel_id=1, source_target_pairs={{0,4},{1,3},{2,6},{3,1},{4,0},{5,7},{6,2},{7,5},{8,12},{9,11},{10,... | collective-permute-start | bytes 540680 | tf_op jit(solution)/shard_map/ppermute | solution.py:947
  81.2 10.1 %collective-permute-start.25 = (bf16[512,512]{1,0:T(8,128)(2,1)S(1)}, bf16[512,512]{1,0:T(8,128)(2,1)S(1)}, u32[]{:S(2)}, u32[]{:S(2)}) collective-permute-start(bf16[512,512]{1,0:T(8,128)(2,1)S(1)} %feed_join_1_1.1.refs_0_.refs_3_.refs_1_), channel_id=1, source_target_pairs={{0,2},{1,5},{2,0},{3,7},{4,6},{5,1},{6,4},{7,3},{8,10},{9,13},{10,... | collective-permute-start | bytes 1572872 | tf_op jit(solution)/shard_map/ppermute | solution.py:889
  83.8 5.0 %collective-permute-start.26 = (bf16[1024,512]{1,0:T(8,128)(2,1)S(1)}, bf16[1024,512]{1,0:T(8,128)(2,1)S(1)}, u32[]{:S(2)}, u32[]{:S(2)}) collective-permute-start(bf16[1024,512]{1,0:T(8,128)(2,1)S(1)} %feed_own.1.refs_1_), channel_id=1, source_target_pairs={{0,1},{1,0},{2,3},{3,2},{4,5},{5,4},{6,7},{7,6},{8,9},{9,8},{10,11... | collective-permute-start | bytes 3145736 | tf_op jit(solution)/shard_map/ppermute | solution.py:552
  85.7 6.8 %collective-permute-start.24 = (bf16[512,512]{1,0:T(8,128)(2,1)S(1)}, bf16[512,512]{1,0:T(8,128)(2,1)S(1)}, u32[]{:S(2)}, u32[]{:S(2)}) collective-permute-start(bf16[512,512]{1,0:T(8,128)(2,1)S(1)} %feed_got_0.1.refs_0_.refs_3_), channel_id=1, source_target_pairs={{0,1},{1,0},{2,3},{3,2},{4,5},{5,4},{6,7},{7,6},{8,9},{9,8},{10,11... | collective-permute-start | bytes 1572872 | tf_op jit(solution)/shard_map/ppermute | solution.py:552
  86.9 8.2 %collective-permute-start.23 = (bf16[352,512]{1,0:T(8,128)(2,1)S(1)}, bf16[352,512]{1,0:T(8,128)(2,1)S(1)}, u32[]{:S(2)}, u32[]{:S(2)}) collective-permute-start(bf16[352,512]{1,0:T(8,128)(2,1)S(1)} %rest_join_1.1.refs_3_.refs_0_), channel_id=1, source_target_pairs={{0,2},{1,5},{2,0},{3,7},{4,6},{5,1},{6,4},{7,3},{8,10},{9,13},{10,... | collective-permute-start | bytes 1081352 | tf_op jit(solution)/shard_map/ppermute | solution.py:889
  91.3 2.0 %collective-permute-start.27 = (bf16[512,512]{1,0:T(8,128)(2,1)S(1)}, bf16[512,512]{1,0:T(8,128)(2,1)S(1)}, u32[]{:S(2)}, u32[]{:S(2)}) collective-permute-start(bf16[512,512]{1,0:T(8,128)(2,1)S(1)} %feed_got_1.1.refs_0_.refs_3_), channel_id=1, source_target_pairs={{0,1},{1,0},{2,3},{3,2},{4,5},{5,4},{6,7},{7,6},{8,9},{9,8},{10,11... | collective-permute-start | bytes 1572872 | tf_op jit(solution)/shard_map/ppermute | solution.py:552

commit v2 on v1

--- a/solution.py
+++ b/solution.py
@@ -934,8 +934,9 @@
             there((size, 2 * cols), LOW),
         )
         got[part] = lax.ppermute(joined[part], AXES, pairs_of(n_dp, steps - 1))
-    rest = add("rest_add_0", rest, rest_got)
-    rest_got = lax.ppermute(rest, AXES, cross_pairs(n_dp, 1))
+        if part == 0:
+            rest = add("rest_add_0", rest, rest_got)
+            rest_got = lax.ppermute(rest, AXES, cross_pairs(n_dp, 1))
     for step in reversed(range(1, steps)):
         for part in range(2):
             name = f"feed_join_{step}_{part}"

time: 96.7 us -> 96.6 us (level)
  waiting for transfers between devices: 18.5 us -> 17.3 us
  starting transfers between devices: 28.9 us -> 30 us
    ppermute x2, waiting for transfers between devices: 3.09 us -> 1.69 us  [local(): got[part] = lax.ppermute(joined[part], AXES, pairs_of(n_dp, steps - 1))]
  transfers between devices with their start and end apart: 28 -> 28, of which waited for: 12 -> 13; matrix products, arithmetic and copies ran while one was open for 0% -> 0% of each run, Pallas kernels for 41% -> 41%
where the time goes in v2:
time: 96.6 us; the launch traced here: 96.4 us
  Pallas kernels  47.8 us (49%)
  starting transfers between devices  30 us (31%)
  waiting for transfers between devices  17.3 us (18%)
  between operations  1.19 us (1%)
    pallas_call x38, Pallas kernels, call(): pl.pallas_call(run, in_specs=[INSIDE] * len(operands) + [ANYWHERE] * (len...  47.8 us
    ppermute x6, starting transfers between devices, across(): lax.ppermute(v, AXES, quad_pairs(n_dp, t + 1))  8.9 us
    ppermute x3, starting transfers between devices, join(): return (joined, lax.ppermute(joined, AXES, pairs_of(n_dp, step - 1)))  5.49 us
    ppermute x6, waiting for transfers between devices, across(): lax.ppermute(v, AXES, quad_pairs(n_dp, t + 1))  5.02 us
    ppermute x2, starting transfers between devices, local(): got[part] = lax.ppermute(joined[part], AXES, pairs_of(n_dp, steps - 1))  3.11 us
    ppermute x1, starting transfers between devices, local(): lax.ppermute(add('feed_add_0', mine, swapped), AXES, pairs_of(n_dp, 0))  2.93 us
    ppermute x2, waiting for transfers between devices, rest_send(): rest_terms.append([lax.ppermute(part, AXES, pairs_of(n_dp, step))])  2.79 us
    ppermute x3, waiting for transfers between devices, join(): return (joined, lax.ppermute(joined, AXES, pairs_of(n_dp, step - 1)))  2.78 us
  transfers between devices with their start and end apart: 28, of which 13 were waited for; matrix products, arithmetic and copies ran while one was open for 0% of the time, Pallas kernels for 41%

profile of v2, /device:TPU:0, one launch (start us, length us, event | category | flops | bytes accessed | tf_op | source)
XLA Modules:
  0.0 96.4 jit_solution(2001129419887547554)
XLA Ops:
  1.2 3.0 %first_norm.1 = (bf16[1024,512]{1,0:T(8,128)(2,1)S(1)}, f32[16,512]{1,0:T(8,128)S(1)}, bf16[1024,128]{1,0:T(8,128)(2,1)S(1)}, bf16[64,1024]{1,0:T(8,128)(2,1)S(1...) custom-call(bf16[1024,512]{1,0:T(8,128)(2,1)} %refs_0_.1, ...), custom_call_target="tpu_custom_call" | custom-call | flops 10000000000 | bytes 1 | tf_op jit(solution)/shard_map/first_norm/pallas_call | solution.py:99
  4.2 5.5 %attention_forward.1 = (bf16[1024,2048]{1,0:T(8,128)(2,1)S(1)}, bf16[64,2048]{1,0:T(8,128)(2,1)S(1)}, f32[64,2048]{1,0:T(8,128)S(1)}, f32[8,2048]{1,0:T(8,128)S(...) custom-call(bf16[1024,512]{1,0:T(8,128)(2,1)S(1)} %get-tuple-element, ...), custom_call_target="tpu_custom_call" | custom-call | flops 10000000000 | bytes 1 | tf_op jit(solution)/shard_map/attention_forward/pallas_call | solution.py:99
  9.7 1.5 %feed_0.1 = (bf16[1024,256]{1,0:T(8,128)(2,1)S(1)}, bf16[1024,256]{1,0:T(8,128)(2,1)S(1)}, f32[1,256]{1,0:T(1,128)S(1)}, bf16[512,512]{1,0:T(8,128)(2,1)S(1)}) custom-call(bf16[1024,512]{1,0:T(8,128)(2,1)S(1)} %get-tuple-element.130.refs_0_, bf16[512,1024]{1,0:T(8,128)(2,1)S(1)} %get-tuple-element.131.refs_1_, ...), custom_call_target="tpu_custom_call" | custom-call | flops 10000000000 | bytes 1 | tf_op jit(solution)/shard_map/feed_0/pallas_call | solution.py:99
  11.7 1.5 %feed_2.1 = (bf16[1024,256]{1,0:T(8,128)(2,1)S(1)}, bf16[1024,256]{1,0:T(8,128)(2,1)S(1)}, f32[1,256]{1,0:T(1,128)S(1)}, bf16[512,512]{1,0:T(8,128)(2,1)S(1)}) custom-call(bf16[1024,512]{1,0:T(8,128)(2,1)S(1)} %get-tuple-element.130.refs_0_, bf16[512,1024]{1,0:T(8,128)(2,1)S(1)} %get-tuple-element.131.refs_1_, ...), custom_call_target="tpu_custom_call" | custom-call | flops 10000000000 | bytes 1 | tf_op jit(solution)/shard_map/feed_2/pallas_call | solution.py:99
  13.4 2.9 %collective-permute-start.4 = (bf16[512,512]{1,0:T(8,128)(2,1)S(1)}, bf16[512,512]{1,0:T(8,128)(2,1)S(1)}, u32[]{:S(2)}, u32[]{:S(2)}) collective-permute-start(bf16[512,512]{1,0:T(8,128)(2,1)S(1)} %feed_add_0.1.refs_7_), channel_id=1, source_target_pairs={{0,2},{1,5},{2,0},{3,7},{4,6},{5,1},{6,4},{7,3},{8,10},{9,13},{10,... | collective-permute-start | bytes 1572872 | tf_op jit(solution)/shard_map/ppermute | solution.py:798
  16.3 1.5 %feed_1.1 = (bf16[1024,256]{1,0:T(8,128)(2,1)S(1)}, bf16[1024,256]{1,0:T(8,128)(2,1)S(1)}, f32[1,256]{1,0:T(1,128)S(1)}, bf16[512,512]{1,0:T(8,128)(2,1)S(1)}) custom-call(bf16[1024,512]{1,0:T(8,128)(2,1)S(1)} %get-tuple-element.130.refs_0_, bf16[512,1024]{1,0:T(8,128)(2,1)S(1)} %get-tuple-element.131.refs_1_, ...), custom_call_target="tpu_custom_call" | custom-call | flops 10000000000 | bytes 1 | tf_op jit(solution)/shard_map/feed_1/pallas_call | solution.py:99
  17.9 1.5 %feed_3.1 = (bf16[1024,256]{1,0:T(8,128)(2,1)S(1)}, bf16[1024,256]{1,0:T(8,128)(2,1)S(1)}, f32[1,256]{1,0:T(1,128)S(1)}, bf16[512,512]{1,0:T(8,128)(2,1)S(1)}) custom-call(bf16[1024,512]{1,0:T(8,128)(2,1)S(1)} %get-tuple-element.130.refs_0_, bf16[512,1024]{1,0:T(8,128)(2,1)S(1)} %get-tuple-element.131.refs_1_, ...), custom_call_target="tpu_custom_call" | custom-call | flops 10000000000 | bytes 1 | tf_op jit(solution)/shard_map/feed_3/pallas_call | solution.py:99
  19.9 1.1 %collective-permute-start.5 = (bf16[512,512]{1,0:T(8,128)(2,1)S(1)}, bf16[512,512]{1,0:T(8,128)(2,1)S(1)}, u32[]{:S(2)}, u32[]{:S(2)}) collective-permute-start(bf16[512,512]{1,0:T(8,128)(2,1)S(1)} %feed_add_1.1.refs_7_), channel_id=1, source_target_pairs={{0,2},{1,5},{2,0},{3,7},{4,6},{5,1},{6,4},{7,3},{8,10},{9,13},{10,... | collective-permute-start | bytes 1572872 | tf_op jit(solution)/shard_map/ppermute | solution.py:802
  21.0 2.8 %feed_4.1 = (bf16[1024,256]{1,0:T(8,128)(2,1)S(1)}, bf16[1024,256]{1,0:T(8,128)(2,1)S(1)}, f32[1,256]{1,0:T(1,128)S(1)}, bf16[1024,256]{1,0:T(8,128)(2,1)S(1)}, ...) custom-call(bf16[1024,512]{1,0:T(8,128)(2,1)S(1)} %get-tuple-element.130.refs_0_, ...), custom_call_target="tpu_custom_call" | custom-call | flops 10000000000 | bytes 1 | tf_op jit(solution)/shard_map/feed_4/pallas_call | solution.py:99
  24.2 3.0 %feed_6.1 = (bf16[1024,256]{1,0:T(8,128)(2,1)S(1)}, bf16[1024,256]{1,0:T(8,128)(2,1)S(1)}, f32[1,256]{1,0:T(1,128)S(1)}, bf16[1024,256]{1,0:T(8,128)(2,1)S(1)}, ...) custom-call(bf16[1024,512]{1,0:T(8,128)(2,1)S(1)} %get-tuple-element.130.refs_0_, ...), custom_call_target="tpu_custom_call" | custom-call | flops 10000000000 | bytes 1 | tf_op jit(solution)/shard_map/feed_6/pallas_call | solution.py:99
  27.2 3.5 %second_norm_back.1 = (f32[1024,512]{1,0:T(8,128)S(1)}, bf16[1024,512]{1,0:T(8,128)(2,1)S(1)}, f32[1,512]{1,0:T(1,128)S(1)}, f32[1,512]{1,0:T(1,128)S(1)}) custom-call(bf16[1024,256]{1,0:T(8,128)(2,1)S(1)} %get-tuple-element.150.refs_0_, bf16[1024,256]{1,0:T(8,128)(2,1)S(1)} %get-tuple-element.151.refs_1_, bf16[1024,256]{1,0:T(8,128)(2,1)S(1)} %get-tuple-element.152.refs_2_, ...), custom_call_target="tpu_custom_call" | custom-call | flops 10000000000 | bytes 1 | tf_op jit(solution)/shard_map/second_norm_back/pallas_call | solution.py:99
  30.9 0.8 collective-permute-start.8
  31.7 5.7 %attention_backward.1 = (bf16[656,1024]{1,0:T(8,128)(2,1)S(1)}, f32[512,512]{1,0:T(8,128)S(1)}) custom-call(bf16[1024,512]{1,0:T(8,128)(2,1)S(1)} %get-tuple-element.159.refs_0_, bf16[1024,2048]{1,0:T(8,128)(2,1)S(1)} %get-tuple-element.136.refs_7_.refs_1_, bf16[64,2048]{1,0:T(8,128)(2,1)S(1)} %get-tuple-element.160.refs_2_, ...), custom_call_target="tpu_custom_call" | custom-call | flops 10000000000 | bytes 1 | tf_op jit(solution)/shard_map/attention_backward/pallas_call | solution.py:99
  37.4 1.2 %projection_grads.1 = (bf16[704,512]{1,0:T(8,128)(2,1)S(1)}, bf16[704,512]{1,0:T(8,128)(2,1)S(1)}) custom-call(bf16[656,1024]{1,0:T(8,128)(2,1)S(1)} %get-tuple-element.168.refs_0_.refs_20_, f32[512,512]{1,0:T(8,128)S(1)} %get-tuple-element.169.refs_1_, bf16[256,512]{1,0:T(8,128)(2,1)S(1)} %get-tuple-element.122.refs_3_.refs_2_.refs_1_, ...), custom_call_target="tpu_custom_call" | custom-call | flops 10000000000 | bytes 1 | tf_op jit(solution)/shard_map/projection_grads/pallas_call | solution.py:99
  38.9 1.3 %collective-permute-done.8.refs_4_ = bf16[512,512]{1,0:T(8,128)(2,1)S(1)} collective-permute-done((bf16[512,512]{1,0:T(8,128)(2,1)S(1)}, bf16[512,512]{1,0:T(8,128)(2,1)S(1)}, u32[]{:S(2)}, u32[]{:S(2)}) %collective-permute-start.8) | collective-permute-done | bytes 524320 | tf_op jit(solution)/shard_map/ppermute | solution.py:826
  40.7 1.6 %collective-permute-start.11 = (bf16[512,128]{1,0:T(8,128)(2,1)S(1)}, bf16[512,128]{1,0:T(8,128)(2,1)S(1)}, u32[]{:S(2)}, u32[]{:S(2)}) collective-permute-start(bf16[512,128]{1,0:T(8,128)(2,1)S(1)} %get-tuple-element.189), channel_id=1, source_target_pairs={{0,8},{1,9},{2,10},{3,11},{4,12},{5,13},{6,14},{7,15},{8,0},{9,1},... | collective-permute-start | bytes 393224 | tf_op jit(solution)/shard_map/ppermute | solution.py:871
  42.3 2.6 %collective-permute-start.12 = (bf16[512,128]{1,0:T(8,128)(2,1)S(1)}, bf16[512,128]{1,0:T(8,128)(2,1)S(1)}, u32[]{:S(2)}, u32[]{:S(2)}) collective-permute-start(bf16[512,128]{1,0:T(8,128)(2,1)S(1)} %get-tuple-element.190), channel_id=1, source_target_pairs={{0,16},{1,17},{2,18},{3,19},{4,20},{5,21},{6,22},{7,23},{8,24},{9,... | collective-permute-start | bytes 393224 | tf_op jit(solution)/shard_map/ppermute | solution.py:871
  45.2 0.7 collective-permute-start.9
  45.9 4.0 %layer_out.1 = (f32[8,128]{1,0:T(8,128)S(1)}, f32[1024,512]{1,0:T(8,128)}) custom-call(bf16[1024,256]{1,0:T(8,128)(2,1)S(1)} %get-tuple-element.137.refs_7_.refs_0_, bf16[1024,256]{1,0:T(8,128)(2,1)S(1)} %get-tuple-element.141.refs_7_.refs_1_, bf16[1024,256]{1,0:T(8,128)(2,1)S(1)} %get-tuple-element.140.refs_2_, ...), custom_call_target="tpu_custom_call" | custom-call | flops 10000000000 | bytes 1 | tf_op jit(solution)/shard_map/layer_out/pallas_call | solution.py:99
  49.9 2.8 %collective-permute-done.9.refs_2_ = bf16[352,512]{1,0:T(8,128)(2,1)S(1)} collective-permute-done((bf16[352,512]{1,0:T(8,128)(2,1)S(1)}, bf16[352,512]{1,0:T(8,128)(2,1)S(1)}, u32[]{:S(2)}, u32[]{:S(2)}) %collective-permute-start.9) | collective-permute-done | bytes 360480 | tf_op jit(solution)/shard_map/ppermute | solution.py:883
  52.8 0.8 collective-permute-start.10
  53.6 1.1 %collective-permute-done.12.refs_2_ = bf16[512,128]{1,0:T(8,128)(2,1)S(1)} collective-permute-done((bf16[512,128]{1,0:T(8,128)(2,1)S(1)}, bf16[512,128]{1,0:T(8,128)(2,1)S(1)}, u32[]{:S(2)}, u32[]{:S(2)}) %collective-permute-start.12) | collective-permute-done | bytes 131104 | tf_op jit(solution)/shard_map/ppermute | solution.py:871
  54.8 2.5 %collective-permute-start.17 = (bf16[512,128]{1,0:T(8,128)(2,1)S(1)}, bf16[512,128]{1,0:T(8,128)(2,1)S(1)}, u32[]{:S(2)}, u32[]{:S(2)}) collective-permute-start(bf16[512,128]{1,0:T(8,128)(2,1)S(1)} %feed_sum.1.refs_4_.refs_0_), channel_id=1, source_target_pairs={{0,24},{1,25},{2,26},{3,27},{4,28},{5,29},{6,30},{7,31},{8,16},{9,... | collective-permute-start | bytes 393224 | tf_op jit(solution)/shard_map/ppermute | solution.py:871
  57.3 1.0 collective-permute-start.16
  58.3 1.0 collective-permute-start.15
  59.4 1.1 %collective-permute-start.14 = (bf16[176,512]{1,0:T(8,128)(2,1)S(1)}, bf16[176,512]{1,0:T(8,128)(2,1)S(1)}, u32[]{:S(2)}, u32[]{:S(2)}) collective-permute-start(bf16[176,512]{1,0:T(8,128)(2,1)S(1)} %rest_sum.1.refs_9_.refs_0_), channel_id=1, source_target_pairs={{0,8},{1,9},{2,10},{3,11},{4,12},{5,13},{6,14},{7,15},{8,0},{9,1},... | collective-permute-start | bytes 540680 | tf_op jit(solution)/shard_map/ppermute | solution.py:924
  60.5 3.1 %first_norm_back.1 = (f32[8,128]{1,0:T(8,128)S(1)}, f32[1024,512]{1,0:T(8,128)}) custom-call(bf16[656,1024]{1,0:T(8,128)(2,1)S(1)} %get-tuple-element.168.refs_0_.refs_20_, bf16[256,512]{1,0:T(8,128)(2,1)S(1)} %get-tuple-element.122.refs_3_.refs_2_.refs_1_, bf16[256,512]{1,0:T(8,128)(2,1)S(1)} %collective-permute-done.refs_4_.refs_3_.refs_2_, ...), custom_call_target="tpu_custom_call" | custom-call | flops 10000000000 | bytes 1 | tf_op jit(solution)/shard_map/first_norm_back/pallas_call | solution.py:99
  63.6 3.8 %collective-permute-done.16.refs_2_ = bf16[512,128]{1,0:T(8,128)(2,1)S(1)} collective-permute-done((bf16[512,128]{1,0:T(8,128)(2,1)S(1)}, bf16[512,128]{1,0:T(8,128)(2,1)S(1)}, u32[]{:S(2)}, u32[]{:S(2)}) %collective-permute-start.16) | collective-permute-done | bytes 131104 | tf_op jit(solution)/shard_map/ppermute | solution.py:871
  67.5 1.5 %collective-permute-start.19 = (bf16[256,512]{1,0:T(8,128)(2,1)S(1)}, bf16[256,512]{1,0:T(8,128)(2,1)S(1)}, u32[]{:S(2)}, u32[]{:S(2)}) collective-permute-start(bf16[256,512]{1,0:T(8,128)(2,1)S(1)} %feed_row_0.1.refs_2_.refs_0_), channel_id=1, source_target_pairs={{0,4},{1,3},{2,6},{3,1},{4,0},{5,7},{6,2},{7,5},{8,12},{9,11},{10,... | collective-permute-start | bytes 786440 | tf_op jit(solution)/shard_map/ppermute | solution.py:936
  69.0 0.6 collective-permute-done.14.refs_1_
  69.6 1.3 %collective-permute-start.18 = (bf16[176,512]{1,0:T(8,128)(2,1)S(1)}, bf16[176,512]{1,0:T(8,128)(2,1)S(1)}, u32[]{:S(2)}, u32[]{:S(2)}) collective-permute-start(bf16[176,512]{1,0:T(8,128)(2,1)S(1)} %rest_add_0.1.refs_4_.refs_0_), channel_id=1, source_target_pairs={{0,16},{1,17},{2,18},{3,19},{4,20},{5,21},{6,22},{7,23},{8,24},{9,... | collective-permute-start | bytes 540680 | tf_op jit(solution)/shard_map/ppermute | solution.py:939
  71.0 1.6 %collective-permute-start.22 = (bf16[256,512]{1,0:T(8,128)(2,1)S(1)}, bf16[256,512]{1,0:T(8,128)(2,1)S(1)}, u32[]{:S(2)}, u32[]{:S(2)}) collective-permute-start(bf16[256,512]{1,0:T(8,128)(2,1)S(1)} %feed_row_1.1.refs_2_.refs_0_), channel_id=1, source_target_pairs={{0,4},{1,3},{2,6},{3,1},{4,0},{5,7},{6,2},{7,5},{8,12},{9,11},{10,... | collective-permute-start | bytes 786440 | tf_op jit(solution)/shard_map/ppermute | solution.py:936
  72.7 1.7 %collective-permute-done.19.refs_1_ = bf16[256,512]{1,0:T(8,128)(2,1)S(1)} collective-permute-done((bf16[256,512]{1,0:T(8,128)(2,1)S(1)}, bf16[256,512]{1,0:T(8,128)(2,1)S(1)}, u32[]{:S(2)}, u32[]{:S(2)}) %collective-permute-start.19) | collective-permute-done | bytes 262176 | tf_op jit(solution)/shard_map/ppermute | solution.py:936
  74.4 1.8 %collective-permute-start.21 = (bf16[512,512]{1,0:T(8,128)(2,1)S(1)}, bf16[512,512]{1,0:T(8,128)(2,1)S(1)}, u32[]{:S(2)}, u32[]{:S(2)}) collective-permute-start(bf16[512,512]{1,0:T(8,128)(2,1)S(1)} %feed_join_1_0.1.refs_0_.refs_1_), channel_id=1, source_target_pairs={{0,2},{1,5},{2,0},{3,7},{4,6},{5,1},{6,4},{7,3},{8,10},{9,13},{10,... | collective-permute-start | bytes 1572872 | tf_op jit(solution)/shard_map/ppermute | solution.py:889
  76.2 1.1 %place_own_0.1 = (f32[8,128]{1,0:T(8,128)S(1)}, f32[512,2048]{1,0:T(8,128)}, f32[2048,512]{1,0:T(8,128)}) custom-call(bf16[512,512]{1,0:T(8,128)(2,1)S(1)} %feed_join_1_0.1.refs_0_.refs_1_, bf16[512,512]{1,0:T(8,128)(2,1)S(1)} %feed_join_1_0.1.refs_0_.refs_1_), custom_call_target="tpu_custom_call" | custom-call | flops 10000000000 | bytes 1 | tf_op jit(solution)/shard_map/place_own_0/pallas_call | solution.py:99
  77.3 1.9 %collective-permute-done.18.refs_1_ = bf16[176,512]{1,0:T(8,128)(2,1)S(1)} collective-permute-done((bf16[176,512]{1,0:T(8,128)(2,1)S(1)}, bf16[176,512]{1,0:T(8,128)(2,1)S(1)}, u32[]{:S(2)}, u32[]{:S(2)}) %collective-permute-start.18) | collective-permute-done | bytes 180256 | tf_op jit(solution)/shard_map/ppermute | solution.py:939
  79.3 1.8 %collective-permute-start.20 = (bf16[176,512]{1,0:T(8,128)(2,1)S(1)}, bf16[176,512]{1,0:T(8,128)(2,1)S(1)}, u32[]{:S(2)}, u32[]{:S(2)}) collective-permute-start(bf16[176,512]{1,0:T(8,128)(2,1)S(1)} %rest_add_1.1.refs_2_.refs_0_), channel_id=1, source_target_pairs={{0,4},{1,3},{2,6},{3,1},{4,0},{5,7},{6,2},{7,5},{8,12},{9,11},{10,... | collective-permute-start | bytes 540680 | tf_op jit(solution)/shard_map/ppermute | solution.py:948
  81.1 1.5 %collective-permute-start.25 = (bf16[512,512]{1,0:T(8,128)(2,1)S(1)}, bf16[512,512]{1,0:T(8,128)(2,1)S(1)}, u32[]{:S(2)}, u32[]{:S(2)}) collective-permute-start(bf16[512,512]{1,0:T(8,128)(2,1)S(1)} %feed_join_1_1.1.refs_0_.refs_3_.refs_1_), channel_id=1, source_target_pairs={{0,2},{1,5},{2,0},{3,7},{4,6},{5,1},{6,4},{7,3},{8,10},{9,13},{10,... | collective-permute-start | bytes 1572872 | tf_op jit(solution)/shard_map/ppermute | solution.py:889
  82.7 1.1 %place_own_1.1 = (f32[8,128]{1,0:T(8,128)S(1)}, f32[512,2048]{1,0:T(8,128)}, f32[2048,512]{1,0:T(8,128)}) custom-call(bf16[512,512]{1,0:T(8,128)(2,1)S(1)} %feed_join_1_1.1.refs_0_.refs_3_.refs_1_, f32[512,2048]{1,0:T(8,128)} %get-tuple-element.195.refs_1_, f32[2048,512]{1,0:T(8,128)} %get-tuple-element.196.refs_2_, ...), custom_call_target="tpu_custom_call", output_to_operand_aliasing={{1}: (1, {}), {2}: (2, {})} | custom-call | flops 10000000000 | bytes 1 | tf_op jit(solution)/shard_map/place_own_1/pallas_call | solution.py:99
  83.9 1.5 %collective-permute-done.21.refs_0_ = bf16[512,512]{1,0:T(8,128)(2,1)S(1)} collective-permute-done((bf16[512,512]{1,0:T(8,128)(2,1)S(1)}, bf16[512,512]{1,0:T(8,128)(2,1)S(1)}, u32[]{:S(2)}, u32[]{:S(2)}) %collective-permute-start.21) | collective-permute-done | bytes 524320 | tf_op jit(solution)/shard_map/ppermute | solution.py:889
  85.6 1.1 %place_got_0.1 = (f32[8,128]{1,0:T(8,128)S(1)}, f32[512,2048]{1,0:T(8,128)}, f32[2048,512]{1,0:T(8,128)}) custom-call(bf16[512,512]{1,0:T(8,128)(2,1)S(1)} %feed_got_0.1.refs_0_.refs_3_, f32[512,2048]{1,0:T(8,128)} %get-tuple-element.198.refs_1_, f32[2048,512]{1,0:T(8,128)} %get-tuple-element.199.refs_2_, ...), custom_call_target="tpu_custom_call", output_to_operand_aliasing={{1}: (1, {}), {2}: (2, {})} | custom-call | flops 30000001024 | bytes 1 | tf_op jit(solution)/shard_map/place_got_0/pallas_call | solution.py:99
  86.7 2.1 %collective-permute-start.23 = (bf16[352,512]{1,0:T(8,128)(2,1)S(1)}, bf16[352,512]{1,0:T(8,128)(2,1)S(1)}, u32[]{:S(2)}, u32[]{:S(2)}) collective-permute-start(bf16[352,512]{1,0:T(8,128)(2,1)S(1)} %rest_join_1.1.refs_3_.refs_0_), channel_id=1, source_target_pairs={{0,2},{1,5},{2,0},{3,7},{4,6},{5,1},{6,4},{7,3},{8,10},{9,13},{10,... | collective-permute-start | bytes 1081352 | tf_op jit(solution)/shard_map/ppermute | solution.py:889
  88.9 1.5 %place_other.1 = (f32[8,128]{1,0:T(8,128)S(1)}, f32[512,2048]{1,0:T(8,128)}, f32[2048,512]{1,0:T(8,128)}) custom-call(bf16[1024,512]{1,0:T(8,128)(2,1)S(1)} %collective-permute-done.26.refs_0_, f32[512,2048]{1,0:T(8,128)} %get-tuple-element.201.refs_1_, f32[2048,512]{1,0:T(8,128)} %get-tuple-element.202.refs_2_, ...), custom_call_target="tpu_custom_call", output_to_operand_aliasing={{1}: (1, {}), {2}: (2, {})} | custom-call | flops 10000000000 | bytes 1 | tf_op jit(solution)/shard_map/place_other/pallas_call | solution.py:99
  90.3 0.9 collective-permute-done.25.refs_0_
  91.3 1.1 %place_got_1.1 = (f32[8,128]{1,0:T(8,128)S(1)}, f32[512,2048]{1,0:T(8,128)}, f32[2048,512]{1,0:T(8,128)}) custom-call(bf16[512,512]{1,0:T(8,128)(2,1)S(1)} %feed_got_1.1.refs_0_.refs_3_, f32[512,2048]{1,0:T(8,128)} %get-tuple-element.204.refs_1_, f32[2048,512]{1,0:T(8,128)} %get-tuple-element.205.refs_2_, ...), custom_call_target="tpu_custom_call", output_to_operand_aliasing={{1}: (1, {}), {2}: (2, {})} | custom-call | flops 10000000000 | bytes 1 | tf_op jit(solution)/shard_map/place_got_1/pallas_call | solution.py:99
  92.4 0.8 collective-permute-done.27.refs_1_
  93.2 1.5 %place_far.1 = (f32[8,128]{1,0:T(8,128)S(1)}, f32[512,2048]{1,0:T(8,128)}, f32[2048,512]{1,0:T(8,128)}) custom-call(bf16[512,512]{1,0:T(8,128)(2,1)S(1)} %collective-permute-done.24.refs_0_, bf16[512,512]{1,0:T(8,128)(2,1)S(1)} %collective-permute-done.27.refs_1_, ...), custom_call_target="tpu_custom_call", output_to_operand_aliasing={{1}: (2, {}), {2}: (3, {})} | custom-call | flops 10000000000 | bytes 1 | tf_op jit(solution)/shard_map/place_far/pallas_call | solution.py:99
  95.1 1.2 %finish.1 = (f32[8,128]{1,0:T(8,128)}, f32[256,512]{1,0:T(8,128)}, f32[256,512]{1,0:T(8,128)}, f32[64,512]{1,0:T(8,128)}, f32[64,512]{1,0:T(8,128)}, /*index=5*/...) custom-call(bf16[352,512]{1,0:T(8,128)(2,1)S(1)} %rest_join_1.1.refs, ...), custom_call_target="tpu_custom_call" | custom-call | flops 10000000000 | bytes 1 | tf_op jit(solution)/shard_map/finish/pallas_call | solution.py:99
  (50 shorter events, 5.0 us)
Async XLA Ops:
  0.6 3.6 %collective-permute-start = (bf16[256,512]{1,0:T(8,128)(2,1)}, bf16[256,512]{1,0:T(8,128)(2,1)S(1)}, u32[]{:S(2)}, u32[]{:S(2)}) collective-permute-start(bf16[256,512]{1,0:T(8,128)(2,1)} %bitcast.18), channel_id=1, source_target_pairs={{0,1},{1,0},{2,3},{3,2},{4,5},{5,4},{6,7},{7,6},{8,9},{9,8},{10,11... | collective-permute-start | bytes 786440 | tf_op jit(solution)/shard_map/ppermute | solution.py:552
  1.2 3.1 %collective-permute-start.1 = (bf16[256,512]{1,0:T(8,128)(2,1)}, bf16[256,512]{1,0:T(8,128)(2,1)S(1)}, u32[]{:S(2)}, u32[]{:S(2)}) collective-permute-start(bf16[256,512]{1,0:T(8,128)(2,1)} %bitcast.20), channel_id=1, source_target_pairs={{0,1},{1,0},{2,3},{3,2},{4,5},{5,4},{6,7},{7,6},{8,9},{9,8},{10,11... | collective-permute-start | bytes 786440 | tf_op jit(solution)/shard_map/ppermute | solution.py:552
  4.2 5.5 %copy-start = (bf16[1024,512]{1,0:T(8,128)(2,1)}, bf16[1024,512]{1,0:T(8,128)(2,1)S(1)}, u32[]{:S(2)}) copy-start(bf16[1024,512]{1,0:T(8,128)(2,1)S(1)} %get-tuple-element.120.refs_1_.refs_6_) | copy-start | bytes 3145732
  11.2 2.0 %collective-permute-start.2 = (bf16[512,512]{1,0:T(8,128)(2,1)S(1)}, bf16[512,512]{1,0:T(8,128)(2,1)S(1)}, u32[]{:S(2)}, u32[]{:S(2)}) collective-permute-start(bf16[512,512]{1,0:T(8,128)(2,1)S(1)} %get-tuple-element.139), channel_id=1, source_target_pairs={{0,1},{1,0},{2,3},{3,2},{4,5},{5,4},{6,7},{7,6},{8,9},{9,8},{10,11... | collective-permute-start | bytes 1572872 | tf_op jit(solution)/shard_map/ppermute | solution.py:552
  13.4 17.3 %collective-permute-start.4 = (bf16[512,512]{1,0:T(8,128)(2,1)S(1)}, bf16[512,512]{1,0:T(8,128)(2,1)S(1)}, u32[]{:S(2)}, u32[]{:S(2)}) collective-permute-start(bf16[512,512]{1,0:T(8,128)(2,1)S(1)} %feed_add_0.1.refs_7_), channel_id=1, source_target_pairs={{0,2},{1,5},{2,0},{3,7},{4,6},{5,1},{6,4},{7,3},{8,10},{9,13},{10,... | collective-permute-start | bytes 1572872 | tf_op jit(solution)/shard_map/ppermute | solution.py:798
  17.8 2.0 %collective-permute-start.3 = (bf16[512,512]{1,0:T(8,128)(2,1)S(1)}, bf16[512,512]{1,0:T(8,128)(2,1)S(1)}, u32[]{:S(2)}, u32[]{:S(2)}) collective-permute-start(bf16[512,512]{1,0:T(8,128)(2,1)S(1)} %get-tuple-element.144), channel_id=1, source_target_pairs={{0,1},{1,0},{2,3},{3,2},{4,5},{5,4},{6,7},{7,6},{8,9},{9,8},{10,11... | collective-permute-start | bytes 1572872 | tf_op jit(solution)/shard_map/ppermute | solution.py:552
  19.9 10.8 %collective-permute-start.5 = (bf16[512,512]{1,0:T(8,128)(2,1)S(1)}, bf16[512,512]{1,0:T(8,128)(2,1)S(1)}, u32[]{:S(2)}, u32[]{:S(2)}) collective-permute-start(bf16[512,512]{1,0:T(8,128)(2,1)S(1)} %feed_add_1.1.refs_7_), channel_id=1, source_target_pairs={{0,2},{1,5},{2,0},{3,7},{4,6},{5,1},{6,4},{7,3},{8,10},{9,13},{10,... | collective-permute-start | bytes 1572872 | tf_op jit(solution)/shard_map/ppermute | solution.py:802
  23.7 6.9 %collective-permute-start.6 = (bf16[1024,512]{1,0:T(8,128)(2,1)S(1)}, bf16[1024,512]{1,0:T(8,128)(2,1)S(1)}, u32[]{:S(2)}, u32[]{:S(2)}) collective-permute-start(bf16[1024,512]{1,0:T(8,128)(2,1)S(1)} %get-tuple-element.165), channel_id=1, source_target_pairs={{0,1},{1,0},{2,3},{3,2},{4,5},{5,4},{6,7},{7,6},{8,9},{9,8},{10,11... | collective-permute-start | bytes 3145736 | tf_op jit(solution)/shard_map/ppermute | solution.py:552
  30.9 9.2 %collective-permute-start.8 = (bf16[512,512]{1,0:T(8,128)(2,1)S(1)}, bf16[512,512]{1,0:T(8,128)(2,1)S(1)}, u32[]{:S(2)}, u32[]{:S(2)}) collective-permute-start(bf16[512,512]{1,0:T(8,128)(2,1)S(1)} %feed_send_1.1.refs_11_), channel_id=1, source_target_pairs={{0,4},{1,3},{2,6},{3,1},{4,0},{5,7},{6,2},{7,5},{8,12},{9,11},{10,... | collective-permute-start | bytes 1572872 | tf_op jit(solution)/shard_map/ppermute | solution.py:826
  38.6 6.5 %collective-permute-start.7 = (bf16[704,512]{1,0:T(8,128)(2,1)S(1)}, bf16[704,512]{1,0:T(8,128)(2,1)S(1)}, u32[]{:S(2)}, u32[]{:S(2)}) collective-permute-start(bf16[704,512]{1,0:T(8,128)(2,1)S(1)} %get-tuple-element.185), channel_id=1, source_target_pairs={{0,1},{1,0},{2,3},{3,2},{4,5},{5,4},{6,7},{7,6},{8,9},{9,8},{10,11... | collective-permute-start | bytes 2162696 | tf_op jit(solution)/shard_map/ppermute | solution.py:552
  40.7 12.9 %collective-permute-start.11 = (bf16[512,128]{1,0:T(8,128)(2,1)S(1)}, bf16[512,128]{1,0:T(8,128)(2,1)S(1)}, u32[]{:S(2)}, u32[]{:S(2)}) collective-permute-start(bf16[512,128]{1,0:T(8,128)(2,1)S(1)} %get-tuple-element.189), channel_id=1, source_target_pairs={{0,8},{1,9},{2,10},{3,11},{4,12},{5,13},{6,14},{7,15},{8,0},{9,1},... | collective-permute-start | bytes 393224 | tf_op jit(solution)/shard_map/ppermute | solution.py:871
  42.3 12.4 %collective-permute-start.12 = (bf16[512,128]{1,0:T(8,128)(2,1)S(1)}, bf16[512,128]{1,0:T(8,128)(2,1)S(1)}, u32[]{:S(2)}, u32[]{:S(2)}) collective-permute-start(bf16[512,128]{1,0:T(8,128)(2,1)S(1)} %get-tuple-element.190), channel_id=1, source_target_pairs={{0,16},{1,17},{2,18},{3,19},{4,20},{5,21},{6,22},{7,23},{8,24},{9,... | collective-permute-start | bytes 393224 | tf_op jit(solution)/shard_map/ppermute | solution.py:871
  44.9 9.8 %collective-permute-start.13 = (bf16[512,128]{1,0:T(8,128)(2,1)S(1)}, bf16[512,128]{1,0:T(8,128)(2,1)S(1)}, u32[]{:S(2)}, u32[]{:S(2)}) collective-permute-start(bf16[512,128]{1,0:T(8,128)(2,1)S(1)} %get-tuple-element.191), channel_id=1, source_target_pairs={{0,24},{1,25},{2,26},{3,27},{4,28},{5,29},{6,30},{7,31},{8,16},{9,... | collective-permute-start | bytes 393224 | tf_op jit(solution)/shard_map/ppermute | solution.py:871
  45.2 7.5 %collective-permute-start.9 = (bf16[352,512]{1,0:T(8,128)(2,1)S(1)}, bf16[352,512]{1,0:T(8,128)(2,1)S(1)}, u32[]{:S(2)}, u32[]{:S(2)}) collective-permute-start(bf16[352,512]{1,0:T(8,128)(2,1)S(1)} %rest_send_0.1.refs_12_), channel_id=1, source_target_pairs={{0,2},{1,5},{2,0},{3,7},{4,6},{5,1},{6,4},{7,3},{8,10},{9,13},{10,... | collective-permute-start | bytes 1081352 | tf_op jit(solution)/shard_map/ppermute | solution.py:883
  52.8 6.5 %collective-permute-start.10 = (bf16[176,512]{1,0:T(8,128)(2,1)S(1)}, bf16[176,512]{1,0:T(8,128)(2,1)S(1)}, u32[]{:S(2)}, u32[]{:S(2)}) collective-permute-start(bf16[176,512]{1,0:T(8,128)(2,1)S(1)} %rest_send_1.1.refs_4_), channel_id=1, source_target_pairs={{0,4},{1,3},{2,6},{3,1},{4,0},{5,7},{6,2},{7,5},{8,12},{9,11},{10,... | collective-permute-start | bytes 540680 | tf_op jit(solution)/shard_map/ppermute | solution.py:883
  54.8 5.7 %copy-start.1 = (bf16[1024,512]{1,0:T(8,128)(2,1)S(1)}, bf16[1024,512]{1,0:T(8,128)(2,1)}, u32[]{:S(2)}) copy-start(bf16[1024,512]{1,0:T(8,128)(2,1)} %copy-done) | copy-start | bytes 3145732
  54.8 8.8 %collective-permute-start.17 = (bf16[512,128]{1,0:T(8,128)(2,1)S(1)}, bf16[512,128]{1,0:T(8,128)(2,1)S(1)}, u32[]{:S(2)}, u32[]{:S(2)}) collective-permute-start(bf16[512,128]{1,0:T(8,128)(2,1)S(1)} %feed_sum.1.refs_4_.refs_0_), channel_id=1, source_target_pairs={{0,24},{1,25},{2,26},{3,27},{4,28},{5,29},{6,30},{7,31},{8,16},{9,... | collective-permute-start | bytes 393224 | tf_op jit(solution)/shard_map/ppermute | solution.py:871
  57.3 10.1 %collective-permute-start.16 = (bf16[512,128]{1,0:T(8,128)(2,1)S(1)}, bf16[512,128]{1,0:T(8,128)(2,1)S(1)}, u32[]{:S(2)}, u32[]{:S(2)}) collective-permute-start(bf16[512,128]{1,0:T(8,128)(2,1)S(1)} %feed_sum.1.refs_4_.refs_0_), channel_id=1, source_target_pairs={{0,16},{1,17},{2,18},{3,19},{4,20},{5,21},{6,22},{7,23},{8,24},{9,... | collective-permute-start | bytes 393224 | tf_op jit(solution)/shard_map/ppermute | solution.py:871
  58.3 9.2 %collective-permute-start.15 = (bf16[512,128]{1,0:T(8,128)(2,1)S(1)}, bf16[512,128]{1,0:T(8,128)(2,1)S(1)}, u32[]{:S(2)}, u32[]{:S(2)}) collective-permute-start(bf16[512,128]{1,0:T(8,128)(2,1)S(1)} %feed_sum.1.refs_4_.refs_0_), channel_id=1, source_target_pairs={{0,8},{1,9},{2,10},{3,11},{4,12},{5,13},{6,14},{7,15},{8,0},{9,1},... | collective-permute-start | bytes 393224 | tf_op jit(solution)/shard_map/ppermute | solution.py:871
  59.4 10.2 %collective-permute-start.14 = (bf16[176,512]{1,0:T(8,128)(2,1)S(1)}, bf16[176,512]{1,0:T(8,128)(2,1)S(1)}, u32[]{:S(2)}, u32[]{:S(2)}) collective-permute-start(bf16[176,512]{1,0:T(8,128)(2,1)S(1)} %rest_sum.1.refs_9_.refs_0_), channel_id=1, source_target_pairs={{0,8},{1,9},{2,10},{3,11},{4,12},{5,13},{6,14},{7,15},{8,0},{9,1},... | collective-permute-start | bytes 540680 | tf_op jit(solution)/shard_map/ppermute | solution.py:924
  67.5 6.8 %collective-permute-start.19 = (bf16[256,512]{1,0:T(8,128)(2,1)S(1)}, bf16[256,512]{1,0:T(8,128)(2,1)S(1)}, u32[]{:S(2)}, u32[]{:S(2)}) collective-permute-start(bf16[256,512]{1,0:T(8,128)(2,1)S(1)} %feed_row_0.1.refs_2_.refs_0_), channel_id=1, source_target_pairs={{0,4},{1,3},{2,6},{3,1},{4,0},{5,7},{6,2},{7,5},{8,12},{9,11},{10,... | collective-permute-start | bytes 786440 | tf_op jit(solution)/shard_map/ppermute | solution.py:936
  69.6 9.6 %collective-permute-start.18 = (bf16[176,512]{1,0:T(8,128)(2,1)S(1)}, bf16[176,512]{1,0:T(8,128)(2,1)S(1)}, u32[]{:S(2)}, u32[]{:S(2)}) collective-permute-start(bf16[176,512]{1,0:T(8,128)(2,1)S(1)} %rest_add_0.1.refs_4_.refs_0_), channel_id=1, source_target_pairs={{0,16},{1,17},{2,18},{3,19},{4,20},{5,21},{6,22},{7,23},{8,24},{9,... | collective-permute-start | bytes 540680 | tf_op jit(solution)/shard_map/ppermute | solution.py:939
  71.0 10.1 %collective-permute-start.22 = (bf16[256,512]{1,0:T(8,128)(2,1)S(1)}, bf16[256,512]{1,0:T(8,128)(2,1)S(1)}, u32[]{:S(2)}, u32[]{:S(2)}) collective-permute-start(bf16[256,512]{1,0:T(8,128)(2,1)S(1)} %feed_row_1.1.refs_2_.refs_0_), channel_id=1, source_target_pairs={{0,4},{1,3},{2,6},{3,1},{4,0},{5,7},{6,2},{7,5},{8,12},{9,11},{10,... | collective-permute-start | bytes 786440 | tf_op jit(solution)/shard_map/ppermute | solution.py:936
  74.4 11.1 %collective-permute-start.21 = (bf16[512,512]{1,0:T(8,128)(2,1)S(1)}, bf16[512,512]{1,0:T(8,128)(2,1)S(1)}, u32[]{:S(2)}, u32[]{:S(2)}) collective-permute-start(bf16[512,512]{1,0:T(8,128)(2,1)S(1)} %feed_join_1_0.1.refs_0_.refs_1_), channel_id=1, source_target_pairs={{0,2},{1,5},{2,0},{3,7},{4,6},{5,1},{6,4},{7,3},{8,10},{9,13},{10,... | collective-permute-start | bytes 1572872 | tf_op jit(solution)/shard_map/ppermute | solution.py:889
  79.3 7.3 %collective-permute-start.20 = (bf16[176,512]{1,0:T(8,128)(2,1)S(1)}, bf16[176,512]{1,0:T(8,128)(2,1)S(1)}, u32[]{:S(2)}, u32[]{:S(2)}) collective-permute-start(bf16[176,512]{1,0:T(8,128)(2,1)S(1)} %rest_add_1.1.refs_2_.refs_0_), channel_id=1, source_target_pairs={{0,4},{1,3},{2,6},{3,1},{4,0},{5,7},{6,2},{7,5},{8,12},{9,11},{10,... | collective-permute-start | bytes 540680 | tf_op jit(solution)/shard_map/ppermute | solution.py:948
  81.1 10.0 %collective-permute-start.25 = (bf16[512,512]{1,0:T(8,128)(2,1)S(1)}, bf16[512,512]{1,0:T(8,128)(2,1)S(1)}, u32[]{:S(2)}, u32[]{:S(2)}) collective-permute-start(bf16[512,512]{1,0:T(8,128)(2,1)S(1)} %feed_join_1_1.1.refs_0_.refs_3_.refs_1_), channel_id=1, source_target_pairs={{0,2},{1,5},{2,0},{3,7},{4,6},{5,1},{6,4},{7,3},{8,10},{9,13},{10,... | collective-permute-start | bytes 1572872 | tf_op jit(solution)/shard_map/ppermute | solution.py:889
  83.8 5.0 %collective-permute-start.26 = (bf16[1024,512]{1,0:T(8,128)(2,1)S(1)}, bf16[1024,512]{1,0:T(8,128)(2,1)S(1)}, u32[]{:S(2)}, u32[]{:S(2)}) collective-permute-start(bf16[1024,512]{1,0:T(8,128)(2,1)S(1)} %feed_own.1.refs_1_), channel_id=1, source_target_pairs={{0,1},{1,0},{2,3},{3,2},{4,5},{5,4},{6,7},{7,6},{8,9},{9,8},{10,11... | collective-permute-start | bytes 3145736 | tf_op jit(solution)/shard_map/ppermute | solution.py:552
  85.5 6.9 %collective-permute-start.24 = (bf16[512,512]{1,0:T(8,128)(2,1)S(1)}, bf16[512,512]{1,0:T(8,128)(2,1)S(1)}, u32[]{:S(2)}, u32[]{:S(2)}) collective-permute-start(bf16[512,512]{1,0:T(8,128)(2,1)S(1)} %feed_got_0.1.refs_0_.refs_3_), channel_id=1, source_target_pairs={{0,1},{1,0},{2,3},{3,2},{4,5},{5,4},{6,7},{7,6},{8,9},{9,8},{10,11... | collective-permute-start | bytes 1572872 | tf_op jit(solution)/shard_map/ppermute | solution.py:552
  86.7 8.3 %collective-permute-start.23 = (bf16[352,512]{1,0:T(8,128)(2,1)S(1)}, bf16[352,512]{1,0:T(8,128)(2,1)S(1)}, u32[]{:S(2)}, u32[]{:S(2)}) collective-permute-start(bf16[352,512]{1,0:T(8,128)(2,1)S(1)} %rest_join_1.1.refs_3_.refs_0_), channel_id=1, source_target_pairs={{0,2},{1,5},{2,0},{3,7},{4,6},{5,1},{6,4},{7,3},{8,10},{9,13},{10,... | collective-permute-start | bytes 1081352 | tf_op jit(solution)/shard_map/ppermute | solution.py:889
  91.2 2.0 %collective-permute-start.27 = (bf16[512,512]{1,0:T(8,128)(2,1)S(1)}, bf16[512,512]{1,0:T(8,128)(2,1)S(1)}, u32[]{:S(2)}, u32[]{:S(2)}) collective-permute-start(bf16[512,512]{1,0:T(8,128)(2,1)S(1)} %feed_got_1.1.refs_0_.refs_3_), channel_id=1, source_target_pairs={{0,1},{1,0},{2,3},{3,2},{4,5},{5,4},{6,7},{7,6},{8,9},{9,8},{10,11... | collective-permute-start | bytes 1572872 | tf_op jit(solution)/shard_map/ppermute | solution.py:552
